TPU v7x, 32 devices: a whole 2x2x4 slice. The times are simulated.
32 devices in a mesh: segment: 2 (over y), ulysses: 8 (over z, x), rep: 2 (over core).
Axes of the slice: x: 2, y: 2, z: 4, core: 2. Of those that a mesh axis runs over, the one named last changes fastest.
Arguments:
- hidden_in: bfloat16 [512, 3072], P('rep'), parts along dimension 0, may hold values from -6 to 6
- assign: int32 [256], replicated, may hold values from 0 to 255, each once
- order: int32 [4], replicated, may hold values from 0 to 3, each once
- w_qkv: bfloat16 [2, 3072, 3, 1024], P('segment', None, None, 'ulysses'), may hold values from -0.109375 to 0.109375
- w_out: bfloat16 [2, 1024, 3072], P('segment', 'ulysses'), may hold values from -0.1875 to 0.1875
- mod_shift: float32 [2, 3072], P('segment'), may hold values from -3 to 3
- mod_scale: float32 [2, 3072], P('segment'), may hold values from -3 to 3
- mod_gate: float32 [2, 3072], P('segment'), may hold values from 1 to 3
- q_gain: float32 [2, 128], P('segment'), may hold values from 0.5 to 2
- k_gain: float32 [2, 128], P('segment'), may hold values from 0.5 to 2
- stale_keys: bfloat16 [2, 512, 1024], P('segment', 'rep', 'ulysses'), parts along dimension 1, may hold values from -6 to 6
- stale_values: bfloat16 [2, 512, 1024], P('segment', 'rep', 'ulysses'), parts along dimension 1, may hold values from -6 to 6
Outputs:
- block_out: bfloat16 [2, 8, 64, 3072], P('segment', 'rep', 'ulysses'), parts along dimension 1
- new_keys: bfloat16 [2, 512, 1024], P('segment', 'rep', 'ulysses'), parts along dimension 1
- new_values: bfloat16 [2, 512, 1024], P('segment', 'rep', 'ulysses'), parts along dimension 1
There are 2 independent parts, one for each index of `rep`. A program takes and returns all parts, laid end to end along the dimension named above; an argument that names none is the same for every part. Nothing has to cross between parts.
Inputs may be any that keep to these rules, and one draw needn't show every extreme that they name: `assign`: a permutation. `order`: a permutation.
All inputs are finite; a program needn't handle non-finite values.
Results may differ from a plain program's by a relative error of at most 0.03.
Values may be sent and summed in bfloat16 or wider, within the bound.
A program may use at most 64 MiB of HBM per device.

v0:
```python
import math

import jax
import jax.numpy as jnp
from jax import lax
from jax.sharding import PartitionSpec as P


def shifted(x, axis, by):
    size = lax.axis_size(axis)
    pairs = [(i, i + by) for i in range(size) if 0 <= i + by < size]
    return lax.ppermute(x, axis, pairs)


def modulate(hidden, offset, factor):
    values = hidden.astype(jnp.float32)
    center = values - jnp.mean(values, axis=-1, keepdims=True)
    spread = jnp.mean(center * center, axis=-1, keepdims=True)
    normed = center * lax.rsqrt(spread + 1e-06)
    return (normed * (1.0 + factor) + offset).astype(jnp.bfloat16)


def rms_gain(values, channel_gain):
    scaled = values * lax.rsqrt(jnp.mean(values * values, axis=-1, keepdims=True) + 1e-06)
    return (scaled * channel_gain).astype(jnp.bfloat16)


def per_device(
    hidden_in,
    assign,
    order,
    w_qkv,
    w_out,
    mod_shift,
    mod_scale,
    mod_gate,
    q_gain,
    k_gain,
    stale_keys,
    stale_values,
):
    segments = lax.axis_size("segment")
    section = lax.axis_index("segment")
    member = lax.axis_index("ulysses")
    model_width = hidden_in.shape[1]
    head_size = q_gain.shape[1]
    tokens = assign.shape[0]
    patch_count = order.shape[0]
    patch_rows = tokens // patch_count
    local_rows = patch_rows // lax.axis_size("ulysses")
    owners = assign.reshape(patch_count, patch_rows)
    weights = w_qkv[0].reshape(model_width, 3 * head_size)
    offset = mod_shift[0]
    factor = mod_scale[0]
    gating = mod_gate[0]
    query_gain = q_gain[0]
    key_gain = k_gain[0]
    out_rows = w_out[0]

    def project(piece):
        return jnp.dot(piece, weights, preferred_element_type=jnp.float32)

    def advance(step_index, carry):
        previous, key_cache, value_cache, results = carry
        arrived = shifted(previous, "segment", 1)
        position = step_index - section
        active = jnp.logical_and(position >= 0, position < patch_count)
        patch_id = order[jnp.clip(position, 0, patch_count - 1)]
        rows_here = owners[patch_id]
        my_rows = lax.dynamic_slice_in_dim(rows_here, member * local_rows, local_rows)
        current = jnp.where(section == 0, hidden_in[my_rows], arrived)
        normed = modulate(current, offset, factor)
        projected = project(lax.all_gather(normed, "ulysses", axis=0, tiled=True))
        queries = rms_gain(projected[:, :head_size], query_gain)
        fresh_keys = rms_gain(projected[:, head_size : 2 * head_size], key_gain)
        fresh_values = projected[:, 2 * head_size :].astype(jnp.bfloat16)
        key_cache = jnp.where(active, key_cache.at[rows_here].set(fresh_keys), key_cache)
        value_cache = jnp.where(active, value_cache.at[rows_here].set(fresh_values), value_cache)
        scores = lax.dot_general(
            queries, key_cache, (((1,), (1,)), ((), ())), preferred_element_type=jnp.float32
        )
        scores = scores / math.sqrt(head_size)
        largest = jnp.max(scores, axis=-1, keepdims=True)
        exponent = jnp.exp(scores - largest)
        probs = (exponent / jnp.sum(exponent, axis=-1, keepdims=True)).astype(jnp.bfloat16)
        attended = jnp.dot(probs, value_cache, preferred_element_type=jnp.float32).astype(
            jnp.bfloat16
        )
        branch = lax.psum_scatter(
            jnp.dot(attended, out_rows, preferred_element_type=jnp.float32).astype(jnp.bfloat16),
            "ulysses",
            scatter_dimension=0,
            tiled=True,
        ).astype(jnp.float32)
        updated = (current.astype(jnp.float32) + gating * branch).astype(jnp.bfloat16)
        results = jnp.where(active, results.at[patch_id].set(updated), results)
        return (updated, key_cache, value_cache, results)

    initial = (
        jnp.zeros((local_rows, model_width), jnp.bfloat16),
        stale_keys[0],
        stale_values[0],
        jnp.zeros((patch_count, local_rows, model_width), jnp.bfloat16),
    )
    final = lax.fori_loop(0, patch_count + segments - 1, advance, initial)
    return (final[3][None], final[1][None], final[2][None])


def solution(mesh):
    placed = (
        P("rep", None),
        P(),
        P(),
        P("segment", None, None, "ulysses"),
        P("segment", "ulysses", None),
        P("segment", None),
        P("segment", None),
        P("segment", None),
        P("segment", None),
        P("segment", None),
        P("segment", "rep", "ulysses"),
        P("segment", "rep", "ulysses"),
    )
    return jax.shard_map(
        per_device,
        mesh=mesh,
        in_specs=placed,
        out_specs=(
            P("segment", "rep", "ulysses", None),
            P("segment", "rep", "ulysses"),
            P("segment", "rep", "ulysses"),
        ),
        check_vma=False,
    )
```

profile of v0, /device:TPU:4, one launch (start us, length us, event | category | flops | bytes accessed | tf_op | source)
XLA Modules:
  0.0 591.2 jit_solution(13381879775744036353)
XLA Ops:
  7.2 4.3 copy.16
  11.5 3.1 copy.17
  15.9 568.0 %while.24 = (s32[]{:T(128)}, bf16[8,3072]{1,0:T(8,128)(2,1)S(1)}, bf16[256,128]{1,0:T(8,128)(2,1)S(1)}, bf16[256,128]{1,0:T(8,128)(2,1)S(1)}, bf16[4,8,3072]{2,1...) while((s32[]{:T(128)}, bf16[8,3072]{1,0:T(8,128)(2,1)S(1)}, ...), condition=%wide.region_11.12_spmd.clone, body=%wide.region_0.11_spmd.clone.sunk | while | flops 210702592 | bytes 8067946 | solution.py:105
  16.0 1.3 collective-permute-start
  17.3 1.2 dynamic_slice.46
  21.9 1.3 broadcast_add_fusion.2
  23.2 1.3 fusion.48
  24.4 2.4 gather_fusion
  28.0 31.3 %all_gather.13 = bf16[64,3072]{1,0:T(8,128)(2,1)S(1)} all-gather(bf16[8,3072]{1,0:T(8,128)(2,1)S(1)} %fusion.51), channel_id=1, replica_groups=mesh['segment'=2,'ulysses'=8,'rep'=2] {'ulysses'}, dimensions={0}, use_global_device_ids=true | all-gather | bytes 442368 | tf_op jit(solution)/shard_map/while/body/eval_jaxpr/all_gather | solution.py:73
  60.9 0.9 scatter_custom_fusion.12
  61.9 1.1 scatter_custom_fusion.13
  63.1 1.0 fusion.53
  64.2 1.2 convolution_convert_fusion.3
  65.5 1.4 and_reduce_fusion.2
  66.8 62.3 %reduce-scatter.2.cloned.1.call-done = bf16[8,3072]{1,0:T(8,128)(2,1)} async-done(((bf16[64,3072]{1,0:T(8,128)(2,1)}), bf16[8,3072]{1,0:T(8,128)(2,1)}) %reduce-scatter.2.cloned.1.call-update) | async-done | bytes 49168 | tf_op jit(solution)/shard_map/while/body/eval_jaxpr/reduce_scatter | solution.py:89
  129.1 2.1 fusion.55
  131.3 1.3 collective-permute-start
  132.6 1.2 dynamic_slice.46
  137.1 1.3 broadcast_add_fusion.2
  138.4 1.3 fusion.48
  139.7 2.4 gather_fusion
  143.3 31.2 %all_gather.13 = bf16[64,3072]{1,0:T(8,128)(2,1)S(1)} all-gather(bf16[8,3072]{1,0:T(8,128)(2,1)S(1)} %fusion.51), channel_id=1, replica_groups=mesh['segment'=2,'ulysses'=8,'rep'=2] {'ulysses'}, dimensions={0}, use_global_device_ids=true | all-gather | bytes 442368 | tf_op jit(solution)/shard_map/while/body/eval_jaxpr/all_gather | solution.py:73
  177.0 1.1 scatter_custom_fusion.13
  178.2 1.0 fusion.53
  179.3 1.2 convolution_convert_fusion.3
  180.6 1.4 and_reduce_fusion.2
  181.9 60.4 %reduce-scatter.2.cloned.1.call-done = bf16[8,3072]{1,0:T(8,128)(2,1)} async-done(((bf16[64,3072]{1,0:T(8,128)(2,1)}), bf16[8,3072]{1,0:T(8,128)(2,1)}) %reduce-scatter.2.cloned.1.call-update) | async-done | bytes 49168 | tf_op jit(solution)/shard_map/while/body/eval_jaxpr/reduce_scatter | solution.py:89
  242.3 2.1 fusion.55
  244.4 1.3 collective-permute-start
  245.7 1.2 dynamic_slice.46
  250.3 1.3 broadcast_add_fusion.2
  251.6 1.3 fusion.48
  252.8 2.4 gather_fusion
  256.4 31.1 %all_gather.13 = bf16[64,3072]{1,0:T(8,128)(2,1)S(1)} all-gather(bf16[8,3072]{1,0:T(8,128)(2,1)S(1)} %fusion.51), channel_id=1, replica_groups=mesh['segment'=2,'ulysses'=8,'rep'=2] {'ulysses'}, dimensions={0}, use_global_device_ids=true | all-gather | bytes 442368 | tf_op jit(solution)/shard_map/while/body/eval_jaxpr/all_gather | solution.py:73
  290.1 1.1 scatter_custom_fusion.13
  291.3 1.0 fusion.53
  292.5 1.2 convolution_convert_fusion.3
  293.7 1.4 and_reduce_fusion.2
  295.1 60.4 %reduce-scatter.2.cloned.1.call-done = bf16[8,3072]{1,0:T(8,128)(2,1)} async-done(((bf16[64,3072]{1,0:T(8,128)(2,1)}), bf16[8,3072]{1,0:T(8,128)(2,1)}) %reduce-scatter.2.cloned.1.call-update) | async-done | bytes 49168 | tf_op jit(solution)/shard_map/while/body/eval_jaxpr/reduce_scatter | solution.py:89
  355.4 2.1 fusion.55
  357.6 1.3 collective-permute-start
  358.9 1.2 dynamic_slice.46
  363.4 1.3 broadcast_add_fusion.2
  364.7 1.3 fusion.48
  366.0 2.4 gather_fusion
  369.6 31.2 %all_gather.13 = bf16[64,3072]{1,0:T(8,128)(2,1)S(1)} all-gather(bf16[8,3072]{1,0:T(8,128)(2,1)S(1)} %fusion.51), channel_id=1, replica_groups=mesh['segment'=2,'ulysses'=8,'rep'=2] {'ulysses'}, dimensions={0}, use_global_device_ids=true | all-gather | bytes 442368 | tf_op jit(solution)/shard_map/while/body/eval_jaxpr/all_gather | solution.py:73
  403.3 1.1 scatter_custom_fusion.13
  404.5 1.0 fusion.53
  405.7 1.2 convolution_convert_fusion.3
  406.9 1.4 and_reduce_fusion.2
  408.3 60.4 %reduce-scatter.2.cloned.1.call-done = bf16[8,3072]{1,0:T(8,128)(2,1)} async-done(((bf16[64,3072]{1,0:T(8,128)(2,1)}), bf16[8,3072]{1,0:T(8,128)(2,1)}) %reduce-scatter.2.cloned.1.call-update) | async-done | bytes 49168 | tf_op jit(solution)/shard_map/while/body/eval_jaxpr/reduce_scatter | solution.py:89
  468.6 2.1 fusion.55
  470.8 1.3 collective-permute-start
  472.1 1.2 dynamic_slice.46
  476.6 1.3 broadcast_add_fusion.2
  477.9 1.3 fusion.48
  479.2 2.4 gather_fusion
  482.8 31.1 %all_gather.13 = bf16[64,3072]{1,0:T(8,128)(2,1)S(1)} all-gather(bf16[8,3072]{1,0:T(8,128)(2,1)S(1)} %fusion.51), channel_id=1, replica_groups=mesh['segment'=2,'ulysses'=8,'rep'=2] {'ulysses'}, dimensions={0}, use_global_device_ids=true | all-gather | bytes 442368 | tf_op jit(solution)/shard_map/while/body/eval_jaxpr/all_gather | solution.py:73
  516.5 1.1 scatter_custom_fusion.13
  517.6 1.0 fusion.53
  518.8 1.2 convolution_convert_fusion.3
  520.0 1.4 and_reduce_fusion.2
  521.4 60.4 %reduce-scatter.2.cloned.1.call-done = bf16[8,3072]{1,0:T(8,128)(2,1)} async-done(((bf16[64,3072]{1,0:T(8,128)(2,1)}), bf16[8,3072]{1,0:T(8,128)(2,1)}) %reduce-scatter.2.cloned.1.call-update) | async-done | bytes 49168 | tf_op jit(solution)/shard_map/while/body/eval_jaxpr/reduce_scatter | solution.py:89
  581.9 2.1 fusion.55
  (114 shorter events, 27.8 us)
Async XLA Ops:
  11.5 3.1 copy-start.5
  11.5 4.5 copy-start
  11.5 4.5 copy-start.2
  11.5 4.5 copy-start.4
  16.0 113.2 %reduce-scatter.2.cloned.1.call-start = ((), (), s32[]{:S(2)}) async-start(), calls=%async_computation.1 | async-start | bytes 442368 | tf_op jit(solution)/shard_map/while/body/eval_jaxpr/reduce_scatter | solution.py:89
  16.0 10.8 %collective-permute-start = (bf16[8,3072]{1,0:T(8,128)(2,1)S(1)}, bf16[8,3072]{1,0:T(8,128)(2,1)S(1)}, u32[]{:S(2)}, u32[]{:S(2)}) collective-permute-start(bf16[8,3072]{1,0:T(8,128)(2,1)S(1)} %broadcast_select_fusion.7), channel_id=1, source_target_pairs={{0,16},{1,17},{2,18},{3,19},{4,20},{5,21},{6,22},{7,23},{8,24},{9,... | collective-permute-start | bytes 147464 | tf_op jit(solution)/shard_map/while/body/eval_jaxpr/ppermute | solution.py:12
  131.3 111.0 %reduce-scatter.2.cloned.1.call-start = ((), (), s32[]{:S(2)}) async-start(), calls=%async_computation.1 | async-start | bytes 442368 | tf_op jit(solution)/shard_map/while/body/eval_jaxpr/reduce_scatter | solution.py:89
  131.3 10.8 %collective-permute-start = (bf16[8,3072]{1,0:T(8,128)(2,1)S(1)}, bf16[8,3072]{1,0:T(8,128)(2,1)S(1)}, u32[]{:S(2)}, u32[]{:S(2)}) collective-permute-start(bf16[8,3072]{1,0:T(8,128)(2,1)S(1)} %broadcast_select_fusion.7), channel_id=1, source_target_pairs={{0,16},{1,17},{2,18},{3,19},{4,20},{5,21},{6,22},{7,23},{8,24},{9,... | collective-permute-start | bytes 147464 | tf_op jit(solution)/shard_map/while/body/eval_jaxpr/ppermute | solution.py:12
  244.4 111.0 %reduce-scatter.2.cloned.1.call-start = ((), (), s32[]{:S(2)}) async-start(), calls=%async_computation.1 | async-start | bytes 442368 | tf_op jit(solution)/shard_map/while/body/eval_jaxpr/reduce_scatter | solution.py:89
  244.4 10.8 %collective-permute-start = (bf16[8,3072]{1,0:T(8,128)(2,1)S(1)}, bf16[8,3072]{1,0:T(8,128)(2,1)S(1)}, u32[]{:S(2)}, u32[]{:S(2)}) collective-permute-start(bf16[8,3072]{1,0:T(8,128)(2,1)S(1)} %broadcast_select_fusion.7), channel_id=1, source_target_pairs={{0,16},{1,17},{2,18},{3,19},{4,20},{5,21},{6,22},{7,23},{8,24},{9,... | collective-permute-start | bytes 147464 | tf_op jit(solution)/shard_map/while/body/eval_jaxpr/ppermute | solution.py:12
  357.6 111.1 %reduce-scatter.2.cloned.1.call-start = ((), (), s32[]{:S(2)}) async-start(), calls=%async_computation.1 | async-start | bytes 442368 | tf_op jit(solution)/shard_map/while/body/eval_jaxpr/reduce_scatter | solution.py:89
  357.6 10.8 %collective-permute-start = (bf16[8,3072]{1,0:T(8,128)(2,1)S(1)}, bf16[8,3072]{1,0:T(8,128)(2,1)S(1)}, u32[]{:S(2)}, u32[]{:S(2)}) collective-permute-start(bf16[8,3072]{1,0:T(8,128)(2,1)S(1)} %broadcast_select_fusion.7), channel_id=1, source_target_pairs={{0,16},{1,17},{2,18},{3,19},{4,20},{5,21},{6,22},{7,23},{8,24},{9,... | collective-permute-start | bytes 147464 | tf_op jit(solution)/shard_map/while/body/eval_jaxpr/ppermute | solution.py:12
  470.8 111.1 %reduce-scatter.2.cloned.1.call-start = ((), (), s32[]{:S(2)}) async-start(), calls=%async_computation.1 | async-start | bytes 442368 | tf_op jit(solution)/shard_map/while/body/eval_jaxpr/reduce_scatter | solution.py:89
  470.8 10.8 %collective-permute-start = (bf16[8,3072]{1,0:T(8,128)(2,1)S(1)}, bf16[8,3072]{1,0:T(8,128)(2,1)S(1)}, u32[]{:S(2)}, u32[]{:S(2)}) collective-permute-start(bf16[8,3072]{1,0:T(8,128)(2,1)S(1)} %broadcast_select_fusion.7), channel_id=1, source_target_pairs={{0,16},{1,17},{2,18},{3,19},{4,20},{5,21},{6,22},{7,23},{8,24},{9,... | collective-permute-start | bytes 147464 | tf_op jit(solution)/shard_map/while/body/eval_jaxpr/ppermute | solution.py:12
  584.0 0.6 copy-start.1
  584.0 0.6 copy-start.3
Sparse Core Ops, SparseCore 0:
  65.6 63.5 reduce-scatter.1
  180.7 61.5 reduce-scatter.1
  293.8 61.5 reduce-scatter.1
  407.0 61.5 reduce-scatter.1
  520.2 61.6 reduce-scatter.1
where the time goes:
time: 595 us; the launch traced here: 591 us
  waiting for transfers between devices  304 us (51%)
  blocking collectives  156 us (26%)
  other arithmetic  55.6 us (9%)
  local copies, waits for them, and re-layouts  32 us (5%)
  between operations  13.7 us (2%)
  matrix products  13.1 us (2%)
  loops' own time  10.3 us (2%)
  starting transfers between devices  6.51 us (1%)
    reduce_scatter x5, waiting for transfers between devices, advance(): lax.psum_scatter(jnp.dot(attended, out_rows, preferred_element_type=jnp.f...  304 us
    all_gather x5, blocking collectives, advance(): projected = project(lax.all_gather(normed, 'ulysses', axis=0, tiled=True))  156 us
  transfers between devices with their start and end apart: 10, of which 5 were waited for; matrix products, arithmetic and copies ran while one was open for 8% of the time, Pallas kernels for 0%

commit v1 on v0

v1 whole, which is shorter than its diff:
```python
import math

import jax
import jax.numpy as jnp
from jax import lax
from jax.sharding import PartitionSpec as P


def modulate(hidden, offset, factor):
    values = hidden.astype(jnp.float32)
    center = values - jnp.mean(values, axis=-1, keepdims=True)
    spread = jnp.mean(center * center, axis=-1, keepdims=True)
    normed = center * lax.rsqrt(spread + 1e-06)
    return (normed * (1.0 + factor) + offset).astype(jnp.bfloat16)


def rms_gain(values, channel_gain):
    scaled = values * lax.rsqrt(jnp.mean(values * values, axis=-1, keepdims=True) + 1e-06)
    return (scaled * channel_gain).astype(jnp.bfloat16)


def per_device(
    hidden_in,
    assign,
    order,
    w_qkv,
    w_out,
    mod_shift,
    mod_scale,
    mod_gate,
    q_gain,
    k_gain,
    stale_keys,
    stale_values,
):
    segments = lax.axis_size("segment")
    members = lax.axis_size("ulysses")
    section = lax.axis_index("segment")
    member = lax.axis_index("ulysses")
    width = hidden_in.shape[1]
    head = q_gain.shape[1]
    tokens = assign.shape[0]
    patches = order.shape[0]
    local = tokens // patches // members
    mine = patches * local
    rows = assign.reshape(patches, members, local).transpose(1, 0, 2).reshape(tokens)
    place = jnp.zeros((patches,), jnp.int32).at[order].set(jnp.arange(patches, dtype=jnp.int32))
    turn = jnp.broadcast_to(place[None, :, None], (members, patches, local)).reshape(tokens)
    fresh_seen = turn[None, :] <= turn[:, None]
    weights = w_qkv[0].reshape(width, 3 * head)
    old_keys = stale_keys[0][rows]
    old_values = stale_values[0][rows]

    state = hidden_in[rows]
    own = lax.dynamic_slice_in_dim(state, member * mine, mine)
    result = None
    for step in range(segments):
        normed = modulate(state, mod_shift[0], mod_scale[0])
        projected = jnp.dot(normed, weights, preferred_element_type=jnp.float32)
        queries = rms_gain(projected[:, :head], q_gain[0])
        keys = rms_gain(projected[:, head : 2 * head], k_gain[0])
        values = projected[:, 2 * head :].astype(jnp.bfloat16)
        both = jnp.concatenate([keys, old_keys], axis=0)
        scores = lax.dot_general(
            queries, both, (((1,), (1,)), ((), ())), preferred_element_type=jnp.float32
        )
        scores = jnp.where(fresh_seen, scores[:, :tokens], scores[:, tokens:]) / math.sqrt(head)
        exponent = jnp.exp(scores - jnp.max(scores, axis=-1, keepdims=True))
        probs = (exponent / jnp.sum(exponent, axis=-1, keepdims=True)).astype(jnp.bfloat16)
        none = jnp.zeros_like(probs)
        split = jnp.concatenate(
            [jnp.where(fresh_seen, probs, none), jnp.where(fresh_seen, none, probs)], axis=1
        )
        attended = jnp.dot(
            split, jnp.concatenate([values, old_values], axis=0), preferred_element_type=jnp.float32
        ).astype(jnp.bfloat16)
        share = jnp.dot(attended, w_out[0], preferred_element_type=jnp.float32)
        branch = lax.psum_scatter(
            share.astype(jnp.bfloat16), "ulysses", scatter_dimension=0, tiled=True
        ).astype(jnp.float32)
        updated = (own.astype(jnp.float32) + mod_gate[0] * branch).astype(jnp.bfloat16)
        if result is None:
            result = (updated, keys, values)
        else:
            result = tuple(
                jnp.where(section == step, new, old)
                for new, old in zip((updated, keys, values), result)
            )
        if step + 1 < segments:
            own = lax.ppermute(updated, "segment", [(i, i + 1) for i in range(segments - 1)])
            state = lax.all_gather(own, "ulysses", axis=0, tiled=True)
    updated, keys, values = result
    back = jnp.zeros((tokens,), jnp.int32).at[rows].set(jnp.arange(tokens, dtype=jnp.int32))
    return (updated.reshape(1, patches, local, width), keys[back][None], values[back][None])


def solution(mesh):
    placed = (
        P("rep", None),
        P(),
        P(),
        P("segment", None, None, "ulysses"),
        P("segment", "ulysses", None),
        P("segment", None),
        P("segment", None),
        P("segment", None),
        P("segment", None),
        P("segment", None),
        P("segment", "rep", "ulysses"),
        P("segment", "rep", "ulysses"),
    )
    return jax.shard_map(
        per_device,
        mesh=mesh,
        in_specs=placed,
        out_specs=(
            P("segment", "rep", "ulysses", None),
            P("segment", "rep", "ulysses"),
            P("segment", "rep", "ulysses"),
        ),
        check_vma=False,
    )
```

time: 595 us -> 231 us (0.39)
  blocking collectives: 156 us -> 0 us
  waiting for transfers between devices: 304 us -> 175 us
  other arithmetic: 55.6 us -> 10 us
  local copies, waits for them, and re-layouts: 32 us -> 16.6 us
  loops' own time: 10.3 us -> 0 us
    reduce_scatter x5 -> x2, waiting for transfers between devices: 304 us -> 125 us  [per_device(): lax.psum_scatter(share.astype(jnp.bfloat16), 'ulysses', scatter_dimension...]
    all_gather x5 -> x0, blocking collectives: 156 us -> none  [advance(): projected = project(lax.all_gather(normed, 'ulysses', axis=0, tiled=True))]
    all_gather x0 -> x1, waiting for transfers between devices: none -> 43.2 us  [per_device(): state = lax.all_gather(own, 'ulysses', axis=0, tiled=True)]
    select_n x20 -> x8, other arithmetic: 20.8 us -> 2.01 us  [the longest x2 1.01 us: per_device(): jnp.where(fresh_seen, probs, none)]
    another operation x1 -> x0, loops' own time: 10.3 us -> none  [per_device(): final = lax.fori_loop(0, patch_count + segments - 1, advance, initial)]
    another operation x5 -> x0, other arithmetic: 6.87 us -> none
    add x5 -> x1, other arithmetic: 6.54 us -> 0.01 us  [modulate(): return (normed * (1.0 + factor) + offset).astype(jnp.bfloat16)]
    ppermute x5 -> x1, waiting for transfers between devices: 0.01 us -> 6.26 us  [per_device(): lax.ppermute(updated, 'segment', [(i, i + 1) for i in range(segments - 1)])]
  transfers between devices with their start and end apart: 10 -> 4, of which waited for: 5 -> 4; matrix products, arithmetic and copies ran while one was open for 8% -> 2% of each run, Pallas kernels for 0% -> 0%
where the time goes in v1:
time: 231 us; the launch traced here: 229 us
  waiting for transfers between devices  175 us (76%)
  local copies, waits for them, and re-layouts  16.6 us (7%)
  between operations  14.2 us (6%)
  matrix products  11.9 us (5%)
  other arithmetic  10 us (4%)
    reduce_scatter x2, waiting for transfers between devices, per_device(): lax.psum_scatter(share.astype(jnp.bfloat16), 'ulysses', scatter_dimension...  125 us
    all_gather x1, waiting for transfers between devices, per_device(): state = lax.all_gather(own, 'ulysses', axis=0, tiled=True)  43.2 us
    unnamed x49, local copies, waits for them, and re-layouts  6.87 us
    ppermute x1, waiting for transfers between devices, per_device(): lax.ppermute(updated, 'segment', [(i, i + 1) for i in range(segments - 1)])  6.26 us
    dot_general x2, matrix products, per_device(): projected = jnp.dot(normed, weights, preferred_element_type=jnp.float32)  5.51 us
    dot_general x2, matrix products, per_device(): share = jnp.dot(attended, w_out[0], preferred_element_type=jnp.float32)  4.99 us
  transfers between devices with their start and end apart: 4, of which 4 were waited for; matrix products, arithmetic and copies ran while one was open for 2% of the time, Pallas kernels for 0%

profile of v1, /device:TPU:4, one launch (start us, length us, event | category | flops | bytes accessed | tf_op | source)
XLA Modules:
  0.0 229.1 jit_solution(12325987217278148040)
XLA Ops:
  7.2 0.0 copy-start
  7.2 0.0 reduce-scatter.3.cloned.1.call-start
  7.2 0.9 reshape.106
  8.1 0.1 reshape.107
  8.2 0.6 copy-done.16
  8.8 0.0 copy-start.10
  8.8 1.6 gather_fusion
  10.4 0.3 convert_reduce_fusion.1
  10.7 0.6 fusion.8
  11.2 0.0 copy-start.11
  11.3 0.0 copy-start.21
  11.3 4.3 %copy.17 = bf16[1,3072,3,128]{1,3,2,0:T(8,128)(2,1)} copy(bf16[1,3072,3,128]{3,1,2,0:T(8,128)(2,1)} %param.15) | data formatting | bytes 4718592 | tf_op args[3]
  15.6 0.0 copy-start.12
  15.6 0.6 copy-done.12
  16.2 0.0 copy-start.19
  16.2 2.8 %fusion.12 = f32[256,384]{1,0:T(8,128)S(1)} fusion(bf16[3072,384]{0,1:T(8,128)(2,1)} %bitcast.23, bf16[256,3072]{1,0:T(8,128)(2,1)S(1)} %gather_fusion, f32[3072]{0:T(1024)S(1)} %bitcast.38, f32[3072]{0:T(1024)S(1)} %bitcast.30, f32[256]{0:T(256)S(1)} %add_rsqrt_fusion.5, f32[256]{0:T(256)S(1)} %broadcast_multiply_fusion.1), kind=kOutput, calls=%fused_computation.25 | convolution fusion | flops 608698368 | bytes 4352000 | tf_op jit(solution)/shard_map/dot_general | solution.py:59
  19.0 0.0 copy-start.3
  19.0 0.1 multiply_reduce_fusion.3
  19.1 0.6 copy-done.5
  19.7 0.9 gather_fusion.1
  20.6 0.6 scatter_custom_fusion
  21.2 0.1 broadcast_in_dim.11
  21.3 0.1 le.15
  21.4 1.0 multiply_convert_fusion.2
  22.4 1.2 fusion.44
  23.6 0.2 fusion.68
  23.8 0.2 fusion.40
  24.0 0.8 compare_select_fusion.4
  24.8 0.7 compare_select_fusion.3
  25.6 1.1 gather_fusion.2
  26.7 3.1 %convolution_convert_fusion.1 = bf16[256,3072]{1,0:T(8,128)(2,1)} fusion(bf16[1,128,3072]{2,1,0:T(8,128)(2,1)} %param.16, bf16[256,256]{1,0:T(8,128)(2,1)} %compare_select_fusion.3, bf16[256,256]{1,0:T(8,128)(2,1)} %get-tuple-element.15, bf16[256,128]{1,0:T(8,128)(2,1)S(1)} %gather_fusion.2, bf16[256,128]{1,0:T(8,128)(2,1)S(1)} %slice.79), kind=kOutput, calls=%fused_computation.12 | convolution fusion | flops 236486656 | bytes 2752512 | tf_op jit(solution)/shard_map/dot_general | solution.py:77
  29.8 0.0 reduce-scatter.3.cloned.1.call-update
  29.9 0.0 copy-start.13
  29.9 0.0 copy-start.22
  29.9 0.0 all-gather.2.cloned.1.call-start
  29.9 66.1 %reduce-scatter.3.cloned.1.call-done = bf16[32,3072]{1,0:T(8,128)(2,1)} async-done(((bf16[256,3072]{1,0:T(8,128)(2,1)}), bf16[32,3072]{1,0:T(8,128)(2,1)}) %reduce-scatter.3.cloned.1.call-update) | async-done | bytes 196624 | tf_op jit(solution)/shard_map/reduce_scatter | solution.py:78
  96.1 1.0 add_convert_fusion.1
  97.1 1.3 collective-permute-start
  98.4 6.3 %collective-permute-done = bf16[32,3072]{1,0:T(8,128)(2,1)S(1)} collective-permute-done((bf16[32,3072]{1,0:T(8,128)(2,1)S(1)}, bf16[32,3072]{1,0:T(8,128)(2,1)S(1)}, u32[]{:S(2)}, u32[]{:S(2)}) %collective-permute-start) | collective-permute-done | bytes 196640 | tf_op jit(solution)/shard_map/ppermute | solution.py:90
  104.6 0.7 copy-done.7
  105.3 0.0 all-gather.2.cloned.1.call-update
  105.3 0.0 reduce-scatter.5.cloned.1.call-start
  105.4 43.2 %all-gather.2.cloned.1.call-done = bf16[256,3072]{1,0:T(8,128)(2,1)} async-done(((bf16[32,3072]{1,0:T(8,128)(2,1)}), bf16[256,3072]{1,0:T(8,128)(2,1)}) %all-gather.2.cloned.1.call-update) | async-done | bytes 1572880 | tf_op jit(solution)/shard_map/all_gather | solution.py:91
  148.6 1.8 convert_reduce_fusion
  150.4 0.1 copy-done.1
  150.5 0.6 fusion.4
  151.1 0.0 copy-start.18
  151.1 0.0 copy-start.20
  151.1 2.8 %fusion.14 = f32[256,384]{1,0:T(8,128)S(1)} fusion(bf16[3072,384]{0,1:T(8,128)(2,1)} %bitcast.24, bf16[256,3072]{1,0:T(8,128)(2,1)S(1)} %copy-done.1, f32[256]{0:T(256)S(1)} %add_rsqrt_fusion.2, f32[256]{0:T(256)S(1)} %broadcast_multiply_fusion, f32[3072]{0:T(1024)S(1)} %bitcast.39, f32[3072]{0:T(1024)S(1)} %bitcast.31), kind=kOutput, calls=%fused_computation.26 | convolution fusion | flops 608698368 | bytes 4352000 | tf_op jit(solution)/shard_map/dot_general | solution.py:59
  153.9 0.1 multiply_reduce_fusion.1
  154.1 0.1 broadcast_select_fusion
  154.2 0.3 fusion.45
  154.5 0.2 fusion.66
  154.7 0.2 fusion.41
  154.9 0.2 compare_select_fusion.1
  155.1 0.1 compare_select_fusion
  155.2 0.0 copy-start.8
  155.2 1.9 convolution_convert_fusion
  157.1 0.0 reduce-scatter.5.cloned.1.call-update
  157.1 1.5 scatter_custom_fusion.1
  158.7 1.5 gather_fusion.3
  160.1 1.5 gather_fusion.4
  161.6 59.2 %reduce-scatter.5.cloned.1.call-done = bf16[32,3072]{1,0:T(8,128)(2,1)} async-done(((bf16[256,3072]{1,0:T(8,128)(2,1)}), bf16[32,3072]{1,0:T(8,128)(2,1)}) %reduce-scatter.5.cloned.1.call-update) | async-done | bytes 196624 | tf_op jit(solution)/shard_map/reduce_scatter | solution.py:78
  220.9 1.7 fusion.43
  (48 shorter events, 0.2 us)
Async XLA Ops:
  7.2 1.6 copy-start
  7.2 88.9 %reduce-scatter.3.cloned.1.call-start = ((), (), s32[]{:S(2)}) async-start(), calls=%async_computation.2 | async-start | bytes 1769472 | tf_op jit(solution)/shard_map/reduce_scatter | solution.py:78
  8.2 0.6 copy-start.16
  8.8 10.9 %copy-start.10 = (s32[1024]{0:T(1024)}, s32[1024]{0:T(1024)S(1)}, u32[]{:S(2)}) copy-start(s32[1024]{0:T(1024)S(1)} %pad_clamp_fusion.1) | copy-start | bytes 12292
  11.2 4.3 %copy-start.11 = (f32[1,3072]{1,0:T(1,128)S(1)}, f32[1,3072]{1,0:T(1,128)}, u32[]{:S(2)}) copy-start(f32[1,3072]{1,0:T(1,128)} %param.18) | copy-start | bytes 36868
  11.3 4.9 %copy-start.21 = (f32[1,3072]{1,0:T(1,128)S(1)}, f32[1,3072]{1,0:T(1,128)}, u32[]{:S(2)}) copy-start(f32[1,3072]{1,0:T(1,128)} %param.17) | copy-start | bytes 36868
  15.6 0.6 copy-start.12
  16.2 3.5 %copy-start.2 = (bf16[1,256,128]{2,1,0:T(8,128)(2,1)S(1)}, bf16[1,256,128]{2,1,0:T(8,128)(2,1)}, u32[]{:S(2)}) copy-start(bf16[1,256,128]{2,1,0:T(8,128)(2,1)} %param.22) | copy-start | bytes 196612
  16.2 4.4 %copy-start.23 = (s32[4]{0:T(128)S(1)}, s32[4]{0:T(128)}, u32[]{:S(2)}) copy-start(s32[4]{0:T(128)} %param.14) | copy-start | bytes 52
  16.2 5.2 %copy-start.17 = (f32[1,128]{1,0:T(1,128)S(1)}, f32[1,128]{1,0:T(1,128)}, u32[]{:S(2)}) copy-start(f32[1,128]{1,0:T(1,128)} %param.21) | copy-start | bytes 1540
  16.2 6.2 %copy-start.19 = (f32[1,128]{1,0:T(1,128)S(1)}, f32[1,128]{1,0:T(1,128)}, u32[]{:S(2)}) copy-start(f32[1,128]{1,0:T(1,128)} %param.20) | copy-start | bytes 1540
  19.0 0.7 copy-start.5
  19.0 6.6 %copy-start.3 = (bf16[1,256,128]{2,1,0:T(8,128)(2,1)S(1)}, bf16[1,256,128]{2,1,0:T(8,128)(2,1)}, u32[]{:S(2)}) copy-start(bf16[1,256,128]{2,1,0:T(8,128)(2,1)} %param.23) | copy-start | bytes 196612
  21.4 2.4 %copy-start.14 = (f32[256]{0:T(256)}, f32[256]{0:T(256)S(1)}, u32[]{:S(2)}) copy-start(f32[256]{0:T(256)S(1)} %get-tuple-element.21) | copy-start | bytes 3076
  25.6 70.5 %copy-start.9 = (f32[1,3072]{1,0:T(1,128)S(1)}, f32[1,3072]{1,0:T(1,128)}, u32[]{:S(2)}) copy-start(f32[1,3072]{1,0:T(1,128)} %param.19) | copy-start | bytes 36868
  29.9 121.2 %copy-start.13 = (f32[1,3072]{1,0:T(1,128)S(1)}, f32[1,3072]{1,0:T(1,128)}, u32[]{:S(2)}) copy-start(f32[1,3072]{1,0:T(1,128)} %copy-done.12) | copy-start | bytes 36868
  29.9 121.2 %copy-start.22 = (f32[1,3072]{1,0:T(1,128)S(1)}, f32[1,3072]{1,0:T(1,128)}, u32[]{:S(2)}) copy-start(f32[1,3072]{1,0:T(1,128)} %param.17) | copy-start | bytes 36868
  29.9 118.7 %all-gather.2.cloned.1.call-start = ((), (), s32[]{:S(2)}) async-start(), calls=%async_computation.3 | async-start | bytes 1769472 | tf_op jit(solution)/shard_map/all_gather | solution.py:91
  97.1 7.6 %collective-permute-start = (bf16[32,3072]{1,0:T(8,128)(2,1)S(1)}, bf16[32,3072]{1,0:T(8,128)(2,1)S(1)}, u32[]{:S(2)}, u32[]{:S(2)}) collective-permute-start(bf16[32,3072]{1,0:T(8,128)(2,1)S(1)} %add_convert_fusion.1), channel_id=1, source_target_pairs={{0,16},{1,17},{2,18},{3,19},{4,20},{5,21},{6,22},{7,23},{8,24},{9,... | collective-permute-start | bytes 589832 | tf_op jit(solution)/shard_map/ppermute | solution.py:90
  104.6 0.7 copy-start.7
  105.3 115.5 %reduce-scatter.5.cloned.1.call-start = ((), (), s32[]{:S(2)}) async-start(), calls=%async_computation.4 | async-start | bytes 1769472 | tf_op jit(solution)/shard_map/reduce_scatter | solution.py:78
  148.6 1.9 copy-start.1
  151.1 3.0 %copy-start.6 = (f32[256,384]{1,0:T(8,128)S(1)}, f32[256,384]{1,0:T(8,128)}, u32[]{:S(2)}) copy-start(f32[256,384]{1,0:T(8,128)} %copy-done.5) | copy-start | bytes 1179652
  151.1 3.0 %copy-start.15 = (f32[256]{0:T(256)S(1)}, f32[256]{0:T(256)}, u32[]{:S(2)}) copy-start(f32[256]{0:T(256)} %copy-done.14) | copy-start | bytes 3076
  151.1 3.0 %copy-start.18 = (f32[1,128]{1,0:T(1,128)S(1)}, f32[1,128]{1,0:T(1,128)}, u32[]{:S(2)}) copy-start(f32[1,128]{1,0:T(1,128)} %param.21) | copy-start | bytes 1540
  151.1 3.1 %copy-start.20 = (f32[1,128]{1,0:T(1,128)S(1)}, f32[1,128]{1,0:T(1,128)}, u32[]{:S(2)}) copy-start(f32[1,128]{1,0:T(1,128)} %param.20) | copy-start | bytes 1540
  153.9 1.3 copy-start.4
  155.2 65.7 %copy-start.8 = (bf16[32,3072]{1,0:T(8,128)(2,1)S(1)}, bf16[32,3072]{1,0:T(8,128)(2,1)}, u32[]{:S(2)}) copy-start(bf16[32,3072]{1,0:T(8,128)(2,1)} %copy-done.7) | copy-start | bytes 589828
Sparse Core Ops, SparseCore 0:
  30.0 66.0 reduce-scatter.2
  105.5 43.0 all-gather.1
  157.2 63.5 reduce-scatter.4

commit v2 on v1

v2 whole, which is shorter than its diff:
```python
import functools
import math

import jax
import jax.numpy as jnp
from jax import lax
from jax.experimental import pallas as pl
from jax.experimental.pallas import tpu as pltpu
from jax.sharding import PartitionSpec as P

MESH = pl.DeviceIdType.MESH
CHUNKS = 4


def kernel(
    segments,
    members,
    hidden,
    weights,
    out_rows,
    shift,
    scale,
    gate,
    q_gain,
    k_gain,
    turn_col,
    turn_row,
    rows_col,
    rows_row,
    stale_keys,
    stale_values,
    result,
    new_keys,
    new_values,
    state,
    queries,
    keys,
    values,
    old_keys,
    old_values,
    attended,
    out_cols,
    updated,
    landed,
    load_sem,
    w_send,
    w_recv,
    a_send,
    a_pass,
    a_recv,
    s_send,
    s_pass,
    s_recv,
    o_send,
    o_recv,
):
    fast = 2 if members % 2 == 0 else 1
    slow = members // fast
    section = lax.axis_index("segment")
    me = lax.axis_index("ulysses")
    a, b = me // fast, lax.rem(me, fast)
    tokens, head = stale_keys.shape
    width = members * state.shape[2]
    mine = tokens // members
    chunk = tokens // CHUNKS
    first = section == 0
    last = section == segments - 1

    def remote(src, dst, send, recv, member, where=None):
        return pltpu.make_async_remote_copy(
            src_ref=src,
            dst_ref=dst,
            send_sem=send,
            recv_sem=recv,
            device_id={"segment": section if where is None else where, "ulysses": member},
            device_id_type=MESH,
        )

    def other(step):
        return lax.rem(me + step, members)

    def slow_peer(step):
        return lax.rem(a + step, slow)

    def fast_peer(step):
        return lax.rem(b + step, fast)

    def load():
        return pltpu.make_async_copy(hidden, state, load_sem)

    @pl.when(first)
    def _():
        load().start()

    barrier = pltpu.get_barrier_semaphore()

    def greet(member, where):
        pl.semaphore_signal(
            barrier,
            inc=1,
            device_id={"segment": where, "ulysses": member},
            device_id_type=MESH,
        )

    for step in range(1, members):
        greet(other(step), section)

    @pl.when(jnp.logical_not(last))
    def _():
        for step in range(slow):
            greet(slow_peer(step) * fast + b, section + 1)

    @pl.when(jnp.logical_not(first))
    def _():
        for step in range(slow):
            greet(slow_peer(step) * fast + b, section - 1)

    sides = jnp.where(first, 0, 1) + jnp.where(last, 0, 1)
    pl.semaphore_wait(barrier, members - 1 + slow * sides)

    my_head = pl.ds(pl.multiple_of(me * head, head), head)

    def w_copy(step):
        return remote(
            out_rows.at[other(step)], out_cols.at[my_head], w_send.at[step], w_recv.at[me], other(step)
        )

    def w_arrival(step):
        origin = other(step)
        place = out_cols.at[pl.ds(pl.multiple_of(origin * head, head), head)]
        return remote(place, place, w_send.at[step], w_recv.at[origin], origin)

    for step in range(1, members):
        w_copy(step).start()
    out_cols[my_head, :] = out_rows[me]

    lane = lax.broadcasted_iota(jnp.int32, (tokens, tokens), 1)
    pick = (rows_col[...] == lane).astype(jnp.float32).astype(jnp.bfloat16)
    old_keys[...] = jnp.dot(pick, stale_keys[...], preferred_element_type=jnp.float32).astype(jnp.bfloat16)
    old_values[...] = jnp.dot(pick, stale_values[...], preferred_element_type=jnp.float32).astype(jnp.bfloat16)

    def piece(origin, r):
        return state.at[origin, pl.ds(pl.multiple_of(r * chunk, chunk), chunk)]

    def s_arrival(origin, r):
        place = piece(origin, r)
        return remote(place, place, s_send.at[0, r], s_recv.at[origin, r], other(1))

    def s_forward(origin_slow, step, r):
        origin = origin_slow * fast + b
        place = piece(origin, r)
        return remote(
            place,
            place,
            s_pass.at[origin_slow, step, r],
            s_recv.at[origin, r],
            a * fast + fast_peer(step),
        )

    @pl.when(first)
    def _():
        load().wait()

    def gain(part, factor):
        square = jnp.mean(part * part, axis=-1, keepdims=True)
        return (part * lax.rsqrt(square + 1e-06) * factor).astype(jnp.bfloat16)

    def project(r, carry):
        @pl.when(jnp.logical_not(first))
        def _():
            for step in range(slow):
                origin_slow = slow_peer(step)
                s_arrival(origin_slow * fast + b, r).wait_recv()
                for hop in range(1, fast):
                    s_forward(origin_slow, hop, r).start()
            for hop in range(1, fast):
                for step in range(slow):
                    s_arrival(slow_peer(step) * fast + fast_peer(hop), r).wait_recv()

        rows = pl.ds(pl.multiple_of(r * chunk, chunk), chunk)
        total = jnp.zeros((chunk, 1), jnp.float32)
        for k in range(members):
            total += jnp.sum(state[k, rows].astype(jnp.float32), axis=-1, keepdims=True)
        mean = total / width
        total = jnp.zeros((chunk, 1), jnp.float32)
        for k in range(members):
            center = state[k, rows].astype(jnp.float32) - mean
            total += jnp.sum(center * center, axis=-1, keepdims=True)
        inverse = lax.rsqrt(total / width + 1e-06)
        projected = jnp.zeros((chunk, 3 * head), jnp.float32)
        for k in range(members):
            center = state[k, rows].astype(jnp.float32) - mean
            part = (center * inverse * (1.0 + scale[k]) + shift[k]).astype(jnp.bfloat16)
            projected += jnp.dot(part, weights[k], preferred_element_type=jnp.float32)
        queries[rows, :] = gain(projected[:, :head], q_gain[...])
        keys[rows, :] = gain(projected[:, head : 2 * head], k_gain[...])
        values[rows, :] = projected[:, 2 * head :].astype(jnp.bfloat16)
        return carry

    lax.fori_loop(0, CHUNKS, project, 0)

    def attend(r, carry):
        rows = pl.ds(pl.multiple_of(r * chunk, chunk), chunk)
        seen = turn_row[...] <= turn_col[rows, :]
        across = (((1,), (1,)), ((), ()))
        asked = queries[rows, :]
        scores = jnp.where(
            seen,
            lax.dot_general(asked, keys[...], across, preferred_element_type=jnp.float32),
            lax.dot_general(asked, old_keys[...], across, preferred_element_type=jnp.float32),
        ) / math.sqrt(head)
        exponent = jnp.exp(scores - jnp.max(scores, axis=-1, keepdims=True))
        probs = exponent / jnp.sum(exponent, axis=-1, keepdims=True)
        fresh = jnp.where(seen, probs, 0.0).astype(jnp.bfloat16)
        stale = jnp.where(seen, 0.0, probs).astype(jnp.bfloat16)
        attended[rows, my_head] = (
            jnp.dot(fresh, values[...], preferred_element_type=jnp.float32)
            + jnp.dot(stale, old_values[...], preferred_element_type=jnp.float32)
        ).astype(jnp.bfloat16)
        return carry

    lax.fori_loop(0, CHUNKS, attend, 0)

    def heads(origin):
        return attended.at[:, pl.ds(pl.multiple_of(origin * head, head), head)]

    def a_copy(step):
        place = heads(me)
        return remote(place, place, a_send.at[step], a_recv.at[me], slow_peer(step) * fast + b)

    def a_forward(origin_slow, step):
        origin = origin_slow * fast + b
        place = heads(origin)
        return remote(
            place, place, a_pass.at[origin_slow, step], a_recv.at[origin], a * fast + fast_peer(step)
        )

    def a_arrival(origin):
        place = heads(origin)
        return remote(place, place, a_send.at[0], a_recv.at[origin], other(1))

    for step in range(1, slow):
        a_copy(step).start()
    for hop in range(1, fast):
        a_forward(a, hop).start()

    row = lax.broadcasted_iota(jnp.int32, (tokens, tokens), 0)
    put = (rows_row[...] == row).astype(jnp.float32).astype(jnp.bfloat16)
    new_keys[...] = jnp.dot(put, keys[...], preferred_element_type=jnp.float32).astype(jnp.bfloat16)
    new_values[...] = jnp.dot(put, values[...], preferred_element_type=jnp.float32).astype(jnp.bfloat16)

    for step in range(1, slow):
        origin_slow = slow_peer(step)
        a_arrival(origin_slow * fast + b).wait_recv()
        for hop in range(1, fast):
            a_forward(origin_slow, hop).start()
    for step in range(1, members):
        w_arrival(step).wait_recv()
    for hop in range(1, fast):
        for step in range(slow):
            a_arrival(slow_peer(step) * fast + fast_peer(hop)).wait_recv()

    def s_copy(step, r):
        rows = pl.ds(pl.multiple_of(r * chunk, chunk), chunk)
        return remote(
            updated.at[rows],
            piece(me, r),
            s_send.at[step, r],
            s_recv.at[me, r],
            slow_peer(step) * fast + b,
            section + 1,
        )

    def finish(r, carry):
        rows = pl.ds(pl.multiple_of(r * chunk, chunk), chunk)
        branch = jnp.dot(attended[rows, :], out_cols[...], preferred_element_type=jnp.float32)
        updated[rows, :] = (state[me, rows].astype(jnp.float32) + gate[me] * branch).astype(jnp.bfloat16)

        @pl.when(jnp.logical_not(last))
        def _():
            for step in range(slow):
                s_copy(step, r).start()

        return carry

    lax.fori_loop(0, CHUNKS, finish, 0)

    def o_copy(step):
        target = other(step)
        return remote(
            updated.at[pl.ds(pl.multiple_of(target * mine, mine), mine)],
            landed.at[me],
            o_send.at[step],
            o_recv.at[me],
            target,
        )

    def o_arrival(step):
        origin = other(step)
        return remote(landed.at[origin], landed.at[origin], o_send.at[step], o_recv.at[origin], origin)

    for step in range(1, members):
        o_copy(step).start()
    landed[me] = updated[pl.ds(pl.multiple_of(me * mine, mine), mine), :]

    for step in range(1, members):
        w_copy(step).wait_send()
    for step in range(1, slow):
        a_copy(step).wait_send()
    for hop in range(1, fast):
        for step in range(slow):
            a_forward(slow_peer(step), hop).wait_send()

    def drain(r, carry):
        @pl.when(jnp.logical_not(last))
        def _():
            for step in range(slow):
                s_copy(step, r).wait_send()

        @pl.when(jnp.logical_not(first))
        def _():
            for step in range(slow):
                for hop in range(1, fast):
                    s_forward(slow_peer(step), hop, r).wait_send()

        return carry

    lax.fori_loop(0, CHUNKS, drain, 0)
    for step in range(1, members):
        o_arrival(step).wait_recv()
    for step in range(1, members):
        o_copy(step).wait_send()
    result[...] = landed[...]


def per_device(
    hidden_in,
    assign,
    order,
    w_qkv,
    w_out,
    mod_shift,
    mod_scale,
    mod_gate,
    q_gain,
    k_gain,
    stale_keys,
    stale_values,
):
    segments = lax.axis_size("segment")
    members = lax.axis_size("ulysses")
    width = hidden_in.shape[1]
    head = q_gain.shape[1]
    tokens = assign.shape[0]
    patches = order.shape[0]
    local = tokens // patches // members
    mine = patches * local
    part = width // members
    fast = 2 if members % 2 == 0 else 1
    slow = members // fast
    rows = assign.reshape(patches, members, local).transpose(1, 0, 2).reshape(tokens)
    place = jnp.sum(
        jnp.where(
            order[None, :] == jnp.arange(patches, dtype=jnp.int32)[:, None],
            jnp.arange(patches, dtype=jnp.int32)[None, :],
            0,
        ),
        axis=1,
    )
    turn = jnp.broadcast_to(place[None, :, None], (members, patches, local)).reshape(tokens)
    hidden = hidden_in[rows].reshape(tokens, members, part).transpose(1, 0, 2)
    weights = w_qkv[0].reshape(members, part, 3 * head)
    out_rows = w_out[0].reshape(head, members, part).transpose(1, 0, 2)
    bf16 = jnp.bfloat16
    inside = pl.BlockSpec(memory_space=pltpu.VMEM)
    dma = pltpu.SemaphoreType.DMA
    result, new_keys, new_values = pl.pallas_call(
        functools.partial(kernel, segments, members),
        out_shape=(
            jax.ShapeDtypeStruct((members, mine, part), bf16),
            jax.ShapeDtypeStruct((tokens, head), bf16),
            jax.ShapeDtypeStruct((tokens, head), bf16),
        ),
        in_specs=[pl.BlockSpec(memory_space=pl.ANY)] + [inside] * 13,
        out_specs=(inside, inside, inside),
        scratch_shapes=[
            pltpu.VMEM((members, tokens, part), bf16),
            pltpu.VMEM((tokens, head), bf16),
            pltpu.VMEM((tokens, head), bf16),
            pltpu.VMEM((tokens, head), bf16),
            pltpu.VMEM((tokens, head), bf16),
            pltpu.VMEM((tokens, head), bf16),
            pltpu.VMEM((tokens, members * head), bf16),
            pltpu.VMEM((members * head, part), bf16),
            pltpu.VMEM((tokens, part), bf16),
            pltpu.VMEM((members, mine, part), bf16),
            dma(()),
            dma((members,)),
            dma((members,)),
            dma((slow,)),
            dma((slow, fast)),
            dma((members,)),
            dma((slow, CHUNKS)),
            dma((slow, fast, CHUNKS)),
            dma((members, CHUNKS)),
            dma((members,)),
            dma((members,)),
        ],
        compiler_params=pltpu.CompilerParams(
            collective_id=0, has_side_effects=True, vmem_limit_bytes=40 * 2**20
        ),
        cost_estimate=pl.CostEstimate(
            flops=2 * tokens * width * 4 * head, bytes_accessed=10**7, transcendentals=tokens * tokens
        ),
    )(
        hidden,
        weights,
        out_rows,
        mod_shift.reshape(members, 1, part),
        mod_scale.reshape(members, 1, part),
        mod_gate.reshape(members, 1, part),
        q_gain,
        k_gain,
        turn[:, None],
        turn[None, :],
        rows[:, None],
        rows[None, :],
        stale_keys[0],
        stale_values[0],
    )
    block_out = result.transpose(1, 0, 2).reshape(1, patches, local, width)
    return (block_out, new_keys[None], new_values[None])


def solution(mesh):
    placed = (
        P("rep", None),
        P(),
        P(),
        P("segment", None, None, "ulysses"),
        P("segment", "ulysses", None),
        P("segment", None),
        P("segment", None),
        P("segment", None),
        P("segment", None),
        P("segment", None),
        P("segment", "rep", "ulysses"),
        P("segment", "rep", "ulysses"),
    )
    return jax.shard_map(
        per_device,
        mesh=mesh,
        in_specs=placed,
        out_specs=(
            P("segment", "rep", "ulysses", None),
            P("segment", "rep", "ulysses"),
            P("segment", "rep", "ulysses"),
        ),
        check_vma=False,
    )
```

time: 231 us -> 128 us (0.55)
  waiting for transfers between devices: 175 us -> 0 us
  Pallas kernels: 0 us -> 88.4 us
  local copies, waits for them, and re-layouts: 16.6 us -> 37.7 us
  between operations: 14.2 us -> 0.76 us
  matrix products: 11.9 us -> 0 us
  other arithmetic: 10 us -> 0.12 us
    reduce_scatter x2 -> x0, waiting for transfers between devices: 125 us -> none  [per_device(): lax.psum_scatter(share.astype(jnp.bfloat16), 'ulysses', scatter_dimension...]
    pallas_call x0 -> x1, Pallas kernels: none -> 88.4 us  [per_device(): pl.pallas_call(functools.partial(kernel, segments, members), out_shape=(j...]
    all_gather x1 -> x0, waiting for transfers between devices: 43.2 us -> none  [per_device(): state = lax.all_gather(own, 'ulysses', axis=0, tiled=True)]
    another operation x0 -> x6, local copies, waits for them, and re-layouts: none -> 16.7 us  [the longest x2 12.8 us: per_device(): weights = w_qkv[0].reshape(members, part, 3 * head)]
    dot_general x6 -> x0, matrix products: 11.9 us -> none  [the longest x2 5.51 us: per_device(): projected = jnp.dot(normed, weights, preferred_element_type=jnp.float32)]
    unnamed x49 -> x35, local copies, waits for them, and re-layouts: 6.87 us -> 13.3 us
    ppermute x1 -> x0, waiting for transfers between devices: 6.26 us -> none  [per_device(): lax.ppermute(updated, 'segment', [(i, i + 1) for i in range(segments - 1)])]
    reduce_sum x8 -> x1, other arithmetic: 3.9 us -> 0.12 us  [per_device(): jnp.sum(jnp.where(order[None, :] == jnp.arange(patches, dtype=jnp.int32)[...]
  transfers between devices with their start and end apart: 4 -> 0, of which waited for: 4 -> 0; matrix products, arithmetic and copies ran while one was open for 2% -> 0% of each run, Pallas kernels for 0% -> 0%
where the time goes in v2:
time: 128 us; the launch traced here: 127 us
  Pallas kernels  88.4 us (69%)
  local copies, waits for them, and re-layouts  37.7 us (29%)
    pallas_call x1, Pallas kernels, per_device(): pl.pallas_call(functools.partial(kernel, segments, members), out_shape=(j...  88.4 us
    unnamed x35, local copies, waits for them, and re-layouts  13.3 us
    another operation x2, local copies, waits for them, and re-layouts, per_device(): weights = w_qkv[0].reshape(members, part, 3 * head)  12.8 us
    gather x2, local copies, waits for them, and re-layouts, per_device(): hidden = hidden_in[rows].reshape(tokens, members, part).transpose(1, 0, 2)  3.18 us

profile of v2, /device:TPU:4, one launch (start us, length us, event | category | flops | bytes accessed | tf_op | source)
XLA Modules:
  0.0 127.0 jit_solution(15189763718406188585)
XLA Ops:
  0.6 0.0 copy-start
  0.6 0.9 reshape.57
  1.5 0.0 copy-start.13
  1.5 0.1 reshape.58
  1.6 0.0 copy-start.14
  1.7 0.5 copy-done.13
  2.1 0.1 copy-done.14
  2.2 0.0 copy-done
  2.2 1.6 %gather_fusion = bf16[256,3072]{1,0:T(8,128)(2,1)S(1)} fusion(bf16[256,3072]{1,0:T(8,128)(2,1)S(1)} %copy-done, s32[1024]{0:T(1024)S(1)} %pad_clamp_fusion), kind=kCustom, calls=%fused_computation | custom fusion | bytes 3146752 | tf_op jit(solution)/shard_map/gather | solution.py:371
  3.8 1.6 %copy.28 = bf16[256,3072]{0,1:T(8,128)(2,1)} copy(bf16[256,3072]{1,0:T(8,128)(2,1)S(1)} %gather_fusion) | data formatting | bytes 3145728 | tf_op jit(solution)/shard_map/gather | solution.py:371
  5.4 1.9 %copy.29 = bf16[256,8,384]{2,0,1:T(8,128)(2,1)S(1)} copy(bf16[256,8,384]{0,2,1:T(8,128)(2,1)} %bitcast.24) | data formatting | bytes 3145728 | tf_op jit(solution)/shard_map/reshape | solution.py:371
  7.3 5.7 %copy.38 = bf16[1,3072,3,128]{3,2,1,0:T(4,128)(2,1)} copy(bf16[1,3072,3,128]{3,1,2,0:T(8,128)(2,1)} %param.15) | data formatting | bytes 4718592 | tf_op jit(solution)/shard_map/reshape;squeeze | solution.py:372
  12.9 7.1 %reshape.72.weights = bf16[8,384,384]{2,1,0:T(8,128)(2,1)} reshape(bf16[1,3072,3,128]{3,2,1,0:T(4,128)(2,1)} %copy.38) | data formatting | bytes 4718592 | tf_op jit(solution)/shard_map/reshape;squeeze | solution.py:372
  20.1 0.0 copy-start.15
  20.1 0.0 copy-start.3
  20.1 0.0 copy-start.4
  20.1 0.0 copy-start.7
  20.1 2.4 %copy.31 = bf16[1,128,3072]{1,2,0:T(8,128)(2,1)} copy(bf16[1,128,3072]{2,1,0:T(8,128)(2,1)} %param.16) | data formatting | bytes 1572864 | tf_op args[4]
  22.4 2.3 %copy.32 = bf16[128,8,384]{2,0,1:T(8,128)(2,1)} copy(bf16[128,8,384]{0,2,1:T(8,128)(2,1)} %bitcast.25) | data formatting | bytes 1572864 | tf_op jit(solution)/shard_map/reshape;squeeze | solution.py:373
  24.8 0.0 copy-done.15
  24.8 0.1 select_reduce_fusion
  24.9 0.1 broadcast_in_dim.30
  25.0 0.1 broadcast_in_dim_reshape.13.turn_col
  25.1 0.1 broadcast_in_dim_reshape.11.turn_row
  25.2 0.8 copy.36.rows_col
  26.0 1.4 %broadcast_in_dim_reshape.12.rows_row = s32[1,256]{1,0:T(1,128)} reshape(s32[8,4,8]{2,1,0:T(4,128)} %copy-done.13) | data formatting | bytes 2048 | tf_op jit(solution)/shard_map/broadcast_in_dim;reshape | solution.py:427
  27.4 0.0 copy-done.3
  27.4 0.0 copy-done.4
  27.4 0.0 copy-done.7
  27.4 0.0 copy-start.1
  27.4 1.7 %copy-done.1 = bf16[8,384,384]{2,1,0:T(8,128)(2,1)S(1)} copy-done((bf16[8,384,384]{2,1,0:T(8,128)(2,1)S(1)}, bf16[8,384,384]{2,1,0:T(8,128)(2,1)}, u32[]{:S(2)}) %copy-start.1) | copy-done | bytes 2359320
  29.0 0.0 copy-start.2
  29.0 1.1 copy-done.2
  30.2 0.0 copy-start.8
  30.2 0.7 copy-done.8
  30.9 0.0 copy-start.9
  30.9 0.7 copy-done.9
  31.6 0.0 copy-start.10
  31.6 0.7 copy-done.10
  32.3 0.0 copy-start.11
  32.3 0.7 copy-done.11
  32.9 0.0 copy-start.12
  32.9 0.7 copy-done.12
  33.6 88.4 %shard_map.139 = (bf16[8,32,384]{2,1,0:T(8,128)(2,1)S(1)}, bf16[256,128]{1,0:T(8,128)(2,1)S(1)}, bf16[256,128]{1,0:T(8,128)(2,1)S(1)}) custom-call(bf16[8,256,384]{2,1,0:T(8,128)(2,1)S(1)} %bitcast.14, bf16[8,384,384]{2,1,0:T(8,128)(2,1)S(1)} %copy-done.1, bf16[8,128,384]{2,1,0:T(8,128)(2,1)S(1)} %bitcast.15, f32[8,1,384]{2,1,0:T(1,128)S(1)} %bitcast.21, ...), custom_call_target="tpu_custom_call" | custom-call | flops 805306368 | bytes 10000000 | tf_op jit(solution)/shard_map/pallas_call | solution.py:377
  122.0 0.0 copy-start.5
  122.0 0.6 copy-done.5
  122.6 0.0 copy-start.6
  122.6 0.6 copy-done.6
  123.3 0.1 copy.37
  123.3 0.8 reshape.63
  124.1 1.5 %copy.42 = bf16[1,256,128]{2,1,0:T(8,128)(2,1)} copy(bf16[1,256,128]{2,1,0:T(8,128)(2,1)} %bitcast.20) | data formatting | bytes 131072
  125.6 1.5 %copy.43 = bf16[1,256,128]{2,1,0:T(8,128)(2,1)} copy(bf16[1,256,128]{2,1,0:T(8,128)(2,1)} %bitcast.19) | data formatting | bytes 131072
  (3 shorter events, 0.0 us)
Async XLA Ops:
  0.6 1.6 %copy-start = (bf16[256,3072]{1,0:T(8,128)(2,1)S(1)}, bf16[256,3072]{1,0:T(8,128)(2,1)}, u32[]{:S(2)}) copy-start(bf16[256,3072]{1,0:T(8,128)(2,1)} %param.12) | copy-start | bytes 4718596
  1.5 0.6 copy-start.13
  1.6 0.6 copy-start.14
  20.1 4.7 %copy-start.15 = (s32[4]{0:T(128)S(1)}, s32[4]{0:T(128)}, u32[]{:S(2)}) copy-start(s32[4]{0:T(128)} %param.14) | copy-start | bytes 52
  20.1 7.3 %copy-start.3 = (bf16[1,256,128]{2,1,0:T(8,128)(2,1)S(1)}, bf16[1,256,128]{2,1,0:T(8,128)(2,1)}, u32[]{:S(2)}) copy-start(bf16[1,256,128]{2,1,0:T(8,128)(2,1)} %param.22) | copy-start | bytes 196612
  20.1 7.3 %copy-start.4 = (bf16[1,256,128]{2,1,0:T(8,128)(2,1)S(1)}, bf16[1,256,128]{2,1,0:T(8,128)(2,1)}, u32[]{:S(2)}) copy-start(bf16[1,256,128]{2,1,0:T(8,128)(2,1)} %param.23) | copy-start | bytes 196612
  20.1 7.3 %copy-start.7 = (f32[1,3072]{1,0:T(1,128)S(1)}, f32[1,3072]{1,0:T(1,128)}, u32[]{:S(2)}) copy-start(f32[1,3072]{1,0:T(1,128)} %param.17) | copy-start | bytes 36868
  27.4 1.7 %copy-start.1 = (bf16[8,384,384]{2,1,0:T(8,128)(2,1)S(1)}, bf16[8,384,384]{2,1,0:T(8,128)(2,1)}, u32[]{:S(2)}) copy-start(bf16[8,384,384]{2,1,0:T(8,128)(2,1)} %reshape.72.weights) | copy-start | bytes 7077892
  29.0 1.1 copy-start.2
  30.2 0.7 copy-start.8
  30.9 0.7 copy-start.9
  31.6 0.7 copy-start.10
  32.3 0.7 copy-start.11
  32.9 0.7 copy-start.12
  122.0 0.6 copy-start.5
  122.6 0.6 copy-start.6

commit v3 on v2

--- a/solution.py
+++ b/solution.py
@@ -15,36 +15,48 @@
 def kernel(
     segments,
     members,
+    patches,
+    order,
+    weights,
     hidden,
-    weights,
     out_rows,
+    shift_in,
+    scale_in,
+    gate_in,
+    q_gain_in,
+    k_gain_in,
+    assign_in,
+    stale_keys_in,
+    stale_values_in,
+    result,
+    new_keys,
+    new_values,
+    raw,
+    state,
+    pick,
+    queries,
+    keys,
+    values,
+    stale_keys,
+    stale_values,
+    old_keys,
+    old_values,
     shift,
     scale,
     gate,
     q_gain,
     k_gain,
-    turn_col,
-    turn_row,
-    rows_col,
-    rows_row,
-    stale_keys,
-    stale_values,
-    result,
-    new_keys,
-    new_values,
-    state,
-    queries,
-    keys,
-    values,
-    old_keys,
-    old_values,
+    assign,
     attended,
     out_cols,
     updated,
     landed,
     load_sem,
+    raw_sem,
     w_send,
     w_recv,
+    w_pass,
+    w_twin,
     a_send,
     a_pass,
     a_recv,
@@ -58,13 +70,22 @@
     slow = members // fast
     section = lax.axis_index("segment")
     me = lax.axis_index("ulysses")
+    core = lax.axis_index("rep")
     a, b = me // fast, lax.rem(me, fast)
     tokens, head = stale_keys.shape
-    width = members * state.shape[2]
+    part = state.shape[2]
+    width = members * part
+    half = head // 2
+    aligned = part % 128 == 0
     mine = tokens // members
     chunk = tokens // CHUNKS
     first = section == 0
     last = section == segments - 1
+
+    def columns(ref, index):
+        if not aligned:
+            return ref.at[index]
+        return ref.at[:, pl.ds(pl.multiple_of(index * part, 128), part)]
 
     def remote(src, dst, send, recv, member, where=None):
         return pltpu.make_async_remote_copy(
@@ -85,12 +106,34 @@
     def fast_peer(step):
         return lax.rem(b + step, fast)
 
-    def load():
-        return pltpu.make_async_copy(hidden, state, load_sem)
+    my_head = pl.ds(pl.multiple_of(me * head, head), head)
+    loads = [
+        pltpu.make_async_copy(src, dst, load_sem.at[i])
+        for i, (src, dst) in enumerate(
+            (
+                (assign_in, assign),
+                (stale_keys_in, stale_keys),
+                (stale_values_in, stale_values),
+                (shift_in, shift),
+                (scale_in, scale),
+                (q_gain_in, q_gain),
+                (k_gain_in, k_gain),
+                (gate_in, gate),
+                (columns(out_rows, me), out_cols.at[my_head]),
+            )
+        )
+    ]
+
+    def load_raw(k):
+        return pltpu.make_async_copy(columns(hidden, k), raw.at[k], raw_sem.at[k])
+
+    for copy in loads:
+        copy.start()
 
     @pl.when(first)
     def _():
-        load().start()
+        for k in range(members):
+            load_raw(k).start()
 
     barrier = pltpu.get_barrier_semaphore()
 
@@ -115,29 +158,69 @@
         for step in range(slow):
             greet(slow_peer(step) * fast + b, section - 1)
 
+    pl.semaphore_signal(
+        barrier, inc=1, device_id={"rep": 1 - core}, device_id_type=MESH
+    )
     sides = jnp.where(first, 0, 1) + jnp.where(last, 0, 1)
-    pl.semaphore_wait(barrier, members - 1 + slow * sides)
-
-    my_head = pl.ds(pl.multiple_of(me * head, head), head)
+    pl.semaphore_wait(barrier, members + slow * sides)
+
+    def w_place(origin, which):
+        return out_cols.at[pl.ds(pl.multiple_of(origin * head + which * half, half), half)]
 
     def w_copy(step):
-        return remote(
-            out_rows.at[other(step)], out_cols.at[my_head], w_send.at[step], w_recv.at[me], other(step)
-        )
+        target = other(step)
+        rows = pl.ds(pl.multiple_of(core * half, half), half)
+        if aligned:
+            piece = out_rows.at[rows, pl.ds(pl.multiple_of(target * part, 128), part)]
+        else:
+            piece = out_rows.at[target, rows]
+        return remote(piece, w_place(me, core), w_send.at[step], w_recv.at[me], target)
 
     def w_arrival(step):
         origin = other(step)
-        place = out_cols.at[pl.ds(pl.multiple_of(origin * head, head), head)]
+        place = w_place(origin, core)
         return remote(place, place, w_send.at[step], w_recv.at[origin], origin)
 
+    def twin_copy(step, which):
+        origin = other(step)
+        place = w_place(origin, which)
+        return pltpu.make_async_remote_copy(
+            src_ref=place,
+            dst_ref=place,
+            send_sem=w_pass.at[step],
+            recv_sem=w_twin.at[origin],
+            device_id={"rep": 1 - core},
+            device_id_type=MESH,
+        )
+
     for step in range(1, members):
         w_copy(step).start()
-    out_cols[my_head, :] = out_rows[me]
+
+    mine_rows = tokens // members
+    local = mine_rows // patches
+
+    def turns(index):
+        patch = lax.rem(index // local, patches)
+        total = jnp.zeros_like(index)
+        for i in range(patches):
+            total += jnp.where(patch == order[i], i, 0)
+        return total
 
     lane = lax.broadcasted_iota(jnp.int32, (tokens, tokens), 1)
-    pick = (rows_col[...] == lane).astype(jnp.float32).astype(jnp.bfloat16)
-    old_keys[...] = jnp.dot(pick, stale_keys[...], preferred_element_type=jnp.float32).astype(jnp.bfloat16)
-    old_values[...] = jnp.dot(pick, stale_values[...], preferred_element_type=jnp.float32).astype(jnp.bfloat16)
+    row = lax.broadcasted_iota(jnp.int32, (tokens, 1), 0)
+    source = lax.rem(row // local, patches) * (tokens // patches) + row // mine_rows * local + lax.rem(row, local)
+    for copy in loads[:1]:
+        copy.wait()
+    chosen = jnp.sum(jnp.where(lane == source, assign[...].astype(jnp.float32), 0.0), axis=1, keepdims=True)
+    pick[...] = (lane.astype(jnp.float32) == chosen).astype(jnp.float32).astype(jnp.bfloat16)
+    for copy in loads[1:]:
+        copy.wait()
+
+    def exact(mask, data):
+        return jnp.dot(mask, data, preferred_element_type=jnp.float32).astype(jnp.bfloat16)
+
+    old_keys[...] = exact(pick[...], stale_keys[...])
+    old_values[...] = exact(pick[...], stale_values[...])
 
     def piece(origin, r):
         return state.at[origin, pl.ds(pl.multiple_of(r * chunk, chunk), chunk)]
@@ -159,11 +242,15 @@
 
     @pl.when(first)
     def _():
-        load().wait()
-
-    def gain(part, factor):
-        square = jnp.mean(part * part, axis=-1, keepdims=True)
-        return (part * lax.rsqrt(square + 1e-06) * factor).astype(jnp.bfloat16)
+        for k in range(members):
+            load_raw(k).wait()
+
+    def gain(data, factor):
+        square = jnp.mean(data * data, axis=-1, keepdims=True)
+        return (data * lax.rsqrt(square + 1e-06) * factor).astype(jnp.bfloat16)
+
+    def vector(ref, k):
+        return ref[:, k * part : (k + 1) * part] if aligned else ref[k]
 
     def project(r, carry):
         @pl.when(jnp.logical_not(first))
@@ -178,6 +265,12 @@
                     s_arrival(slow_peer(step) * fast + fast_peer(hop), r).wait_recv()
 
         rows = pl.ds(pl.multiple_of(r * chunk, chunk), chunk)
+
+        @pl.when(first)
+        def _():
+            for k in range(members):
+                state[k, rows] = exact(pick[rows, :], raw[k])
+
         total = jnp.zeros((chunk, 1), jnp.float32)
         for k in range(members):
             total += jnp.sum(state[k, rows].astype(jnp.float32), axis=-1, keepdims=True)
@@ -190,8 +283,10 @@
         projected = jnp.zeros((chunk, 3 * head), jnp.float32)
         for k in range(members):
             center = state[k, rows].astype(jnp.float32) - mean
-            part = (center * inverse * (1.0 + scale[k]) + shift[k]).astype(jnp.bfloat16)
-            projected += jnp.dot(part, weights[k], preferred_element_type=jnp.float32)
+            normed = (center * inverse * (1.0 + vector(scale, k)) + vector(shift, k)).astype(jnp.bfloat16)
+            projected += jnp.dot(
+                normed, weights[k * part : (k + 1) * part, :], preferred_element_type=jnp.float32
+            )
         queries[rows, :] = gain(projected[:, :head], q_gain[...])
         keys[rows, :] = gain(projected[:, head : 2 * head], k_gain[...])
         values[rows, :] = projected[:, 2 * head :].astype(jnp.bfloat16)
@@ -201,7 +296,9 @@
 
     def attend(r, carry):
         rows = pl.ds(pl.multiple_of(r * chunk, chunk), chunk)
-        seen = turn_row[...] <= turn_col[rows, :]
+        asking = lax.broadcasted_iota(jnp.int32, (chunk, tokens), 0) + r * chunk
+        asked_of = lax.broadcasted_iota(jnp.int32, (chunk, tokens), 1)
+        seen = turns(asked_of) <= turns(asking)
         across = (((1,), (1,)), ((), ()))
         asked = queries[rows, :]
         scores = jnp.where(
@@ -244,10 +341,13 @@
     for hop in range(1, fast):
         a_forward(a, hop).start()
 
-    row = lax.broadcasted_iota(jnp.int32, (tokens, tokens), 0)
-    put = (rows_row[...] == row).astype(jnp.float32).astype(jnp.bfloat16)
-    new_keys[...] = jnp.dot(put, keys[...], preferred_element_type=jnp.float32).astype(jnp.bfloat16)
-    new_values[...] = jnp.dot(put, values[...], preferred_element_type=jnp.float32).astype(jnp.bfloat16)
+    back = (((0,), (0,)), ((), ()))
+    new_keys[...] = lax.dot_general(
+        pick[...], keys[...], back, preferred_element_type=jnp.float32
+    ).astype(jnp.bfloat16)
+    new_values[...] = lax.dot_general(
+        pick[...], values[...], back, preferred_element_type=jnp.float32
+    ).astype(jnp.bfloat16)
 
     for step in range(1, slow):
         origin_slow = slow_peer(step)
@@ -256,9 +356,13 @@
             a_forward(origin_slow, hop).start()
     for step in range(1, members):
         w_arrival(step).wait_recv()
+        twin_copy(step, core).start()
     for hop in range(1, fast):
         for step in range(slow):
             a_arrival(slow_peer(step) * fast + fast_peer(hop)).wait_recv()
+    for step in range(1, members):
+        twin_copy(step, 1 - core).wait_recv()
+    my_gate = gate[:, pl.ds(pl.multiple_of(me * part, 128), part)] if aligned else gate[me]
 
     def s_copy(step, r):
         rows = pl.ds(pl.multiple_of(r * chunk, chunk), chunk)
@@ -274,7 +378,7 @@
     def finish(r, carry):
         rows = pl.ds(pl.multiple_of(r * chunk, chunk), chunk)
         branch = jnp.dot(attended[rows, :], out_cols[...], preferred_element_type=jnp.float32)
-        updated[rows, :] = (state[me, rows].astype(jnp.float32) + gate[me] * branch).astype(jnp.bfloat16)
+        updated[rows, :] = (state[me, rows].astype(jnp.float32) + my_gate * branch).astype(jnp.bfloat16)
 
         @pl.when(jnp.logical_not(last))
         def _():
@@ -305,6 +409,7 @@
 
     for step in range(1, members):
         w_copy(step).wait_send()
+        twin_copy(step, core).wait_send()
     for step in range(1, slow):
         a_copy(step).wait_send()
     for hop in range(1, fast):
@@ -330,7 +435,11 @@
         o_arrival(step).wait_recv()
     for step in range(1, members):
         o_copy(step).wait_send()
-    result[...] = landed[...]
+    if aligned:
+        for k in range(members):
+            result[:, k * part : (k + 1) * part] = landed[k]
+    else:
+        result[...] = landed[...]
 
 
 def per_device(
@@ -358,43 +467,45 @@
     part = width // members
     fast = 2 if members % 2 == 0 else 1
     slow = members // fast
-    rows = assign.reshape(patches, members, local).transpose(1, 0, 2).reshape(tokens)
-    place = jnp.sum(
-        jnp.where(
-            order[None, :] == jnp.arange(patches, dtype=jnp.int32)[:, None],
-            jnp.arange(patches, dtype=jnp.int32)[None, :],
-            0,
-        ),
-        axis=1,
-    )
-    turn = jnp.broadcast_to(place[None, :, None], (members, patches, local)).reshape(tokens)
-    hidden = hidden_in[rows].reshape(tokens, members, part).transpose(1, 0, 2)
-    weights = w_qkv[0].reshape(members, part, 3 * head)
-    out_rows = w_out[0].reshape(head, members, part).transpose(1, 0, 2)
+    aligned = part % 128 == 0
+
+    def blocks(array):
+        if aligned:
+            return array
+        return array.reshape(array.shape[0], members, part).transpose(1, 0, 2)
+
+    vectors = (1, width) if aligned else (members, 1, part)
+    shaped = (mine, width) if aligned else (members, mine, part)
     bf16 = jnp.bfloat16
     inside = pl.BlockSpec(memory_space=pltpu.VMEM)
     dma = pltpu.SemaphoreType.DMA
     result, new_keys, new_values = pl.pallas_call(
-        functools.partial(kernel, segments, members),
+        functools.partial(kernel, segments, members, patches),
         out_shape=(
-            jax.ShapeDtypeStruct((members, mine, part), bf16),
+            jax.ShapeDtypeStruct(shaped, bf16),
             jax.ShapeDtypeStruct((tokens, head), bf16),
             jax.ShapeDtypeStruct((tokens, head), bf16),
         ),
-        in_specs=[pl.BlockSpec(memory_space=pl.ANY)] + [inside] * 13,
+        in_specs=[pl.BlockSpec(memory_space=pltpu.SMEM), inside] + [pl.BlockSpec(memory_space=pl.ANY)] * 10,
         out_specs=(inside, inside, inside),
         scratch_shapes=[
             pltpu.VMEM((members, tokens, part), bf16),
-            pltpu.VMEM((tokens, head), bf16),
-            pltpu.VMEM((tokens, head), bf16),
-            pltpu.VMEM((tokens, head), bf16),
-            pltpu.VMEM((tokens, head), bf16),
-            pltpu.VMEM((tokens, head), bf16),
+            pltpu.VMEM((members, tokens, part), bf16),
+            pltpu.VMEM((tokens, tokens), bf16),
+        ]
+        + [pltpu.VMEM((tokens, head), bf16)] * 7
+        + [pltpu.VMEM(vectors, jnp.float32)] * 3
+        + [pltpu.VMEM((1, head), jnp.float32)] * 2
+        + [
+            pltpu.VMEM((1, tokens), jnp.int32),
             pltpu.VMEM((tokens, members * head), bf16),
             pltpu.VMEM((members * head, part), bf16),
             pltpu.VMEM((tokens, part), bf16),
             pltpu.VMEM((members, mine, part), bf16),
-            dma(()),
+            dma((9,)),
+            dma((members,)),
+            dma((members,)),
+            dma((members,)),
             dma((members,)),
             dma((members,)),
             dma((slow,)),
@@ -413,22 +524,22 @@
             flops=2 * tokens * width * 4 * head, bytes_accessed=10**7, transcendentals=tokens * tokens
         ),
     )(
-        hidden,
-        weights,
-        out_rows,
-        mod_shift.reshape(members, 1, part),
-        mod_scale.reshape(members, 1, part),
-        mod_gate.reshape(members, 1, part),
+        order,
+        w_qkv[0].reshape(width, 3 * head),
+        blocks(hidden_in),
+        blocks(w_out[0]),
+        blocks(mod_shift),
+        blocks(mod_scale),
+        blocks(mod_gate),
         q_gain,
         k_gain,
-        turn[:, None],
-        turn[None, :],
-        rows[:, None],
-        rows[None, :],
+        assign[None, :],
         stale_keys[0],
         stale_values[0],
     )
-    block_out = result.transpose(1, 0, 2).reshape(1, patches, local, width)
+    if not aligned:
+        result = result.transpose(1, 0, 2)
+    block_out = result.reshape(1, patches, local, width)
     return (block_out, new_keys[None], new_values[None])
 
 

time: 128 us -> 96.6 us (0.75)
  local copies, waits for them, and re-layouts: 37.7 us -> 10.7 us
  Pallas kernels: 88.4 us -> 84.8 us
    another operation x6 -> x1, local copies, waits for them, and re-layouts: 16.7 us -> 3.06 us  [per_device(): w_qkv[0].reshape(width, 3 * head)]
    unnamed x35 -> x26, local copies, waits for them, and re-layouts: 13.3 us -> 7.65 us
    reshape x5 -> x0, local copies, waits for them, and re-layouts: 4.41 us -> none  [the longest x1 1.87 us: per_device(): hidden = hidden_in[rows].reshape(tokens, members, part).transpose(1, 0, 2)]
    pallas_call x1, Pallas kernels: 88.4 us -> 84.8 us  [per_device(): pl.pallas_call(functools.partial(kernel, segments, members, patches), out...]
    gather x2 -> x0, local copies, waits for them, and re-layouts: 3.18 us -> none  [per_device(): hidden = hidden_in[rows].reshape(tokens, members, part).transpose(1, 0, 2)]
where the time goes in v3:
time: 96.6 us; the launch traced here: 96.4 us
  Pallas kernels  84.8 us (88%)
  local copies, waits for them, and re-layouts  10.7 us (11%)
    pallas_call x1, Pallas kernels, per_device(): pl.pallas_call(functools.partial(kernel, segments, members, patches), out...  84.8 us
    unnamed x26, local copies, waits for them, and re-layouts  7.65 us
    another operation x1, local copies, waits for them, and re-layouts, per_device(): w_qkv[0].reshape(width, 3 * head)  3.06 us

profile of v3, /device:TPU:4, one launch (start us, length us, event | category | flops | bytes accessed | tf_op | source)
XLA Modules:
  0.0 96.4 jit_solution(9336038249221588707)
XLA Ops:
  0.6 4.3 %copy.16 = bf16[1,3072,3,128]{1,3,2,0:T(8,128)(2,1)} copy(bf16[1,3072,3,128]{3,1,2,0:T(8,128)(2,1)} %param.15) | data formatting | bytes 4718592 | tf_op args[3]
  4.9 0.0 copy-start.1
  4.9 0.0 copy-start.2
  4.9 0.0 copy-start.3
  4.9 0.0 copy-start.4
  4.9 0.0 copy-start.5
  4.9 0.0 copy-start.6
  4.9 0.0 copy-start.7
  4.9 0.0 copy-start.8
  5.0 0.0 copy-start.9
  5.0 0.0 copy-start.10
  5.0 3.1 %copy.17.weights = bf16[3072,384]{1,0:T(8,128)(2,1)S(1)} copy(bf16[3072,384]{0,1:T(8,128)(2,1)} %bitcast.15) | data formatting | bytes 4718592 | tf_op jit(solution)/shard_map/reshape;squeeze | solution.py:528
  8.1 0.0 copy-done.1
  8.1 0.0 copy-done.2
  8.1 0.0 copy-done.3
  8.1 0.0 copy-done.4
  8.1 0.0 copy-done.5
  8.1 0.0 copy-done.6
  8.1 0.0 copy-done.7
  8.1 0.0 copy-done.8
  8.1 0.0 copy-done.9
  8.1 0.0 copy-done.10
  8.2 0.0 copy-start
  8.2 1.4 %copy-done = bf16[256,3072]{1,0:T(8,128)(2,1)S(1)} copy-done((bf16[256,3072]{1,0:T(8,128)(2,1)S(1)}, bf16[256,3072]{1,0:T(8,128)(2,1)}, u32[]{:S(2)}) %copy-start) | copy-done | bytes 1572888
  9.6 84.8 %shard_map.139 = (bf16[32,3072]{1,0:T(8,128)(2,1)S(1)}, bf16[256,128]{1,0:T(8,128)(2,1)S(1)}, bf16[256,128]{1,0:T(8,128)(2,1)S(1)}) custom-call(s32[4]{0:T(128)S(1)} %copy-done.8, bf16[3072,384]{1,0:T(8,128)(2,1)S(1)} %copy.17.weights, bf16[256,3072]{1,0:T(8,128)(2,1)S(1)} %copy-done, bf16[128,3072]{1,0:T(8,128)(2,1)S(1)} %bitcast.8, ...), custom_call_target="tpu_custom_call" | custom-call | flops 805306368 | bytes 10000000 | tf_op jit(solution)/shard_map/pallas_call | solution.py:482
  94.4 0.7 copy.21
  95.1 0.6 copy.22
  95.7 0.6 copy.23
Async XLA Ops:
  4.9 3.2 %copy-start.1 = (bf16[1,128,3072]{2,1,0:T(8,128)(2,1)S(1)}, bf16[1,128,3072]{2,1,0:T(8,128)(2,1)}, u32[]{:S(2)}) copy-start(bf16[1,128,3072]{2,1,0:T(8,128)(2,1)} %param.16) | copy-start | bytes 2359300
  4.9 3.2 %copy-start.2 = (bf16[1,256,128]{2,1,0:T(8,128)(2,1)S(1)}, bf16[1,256,128]{2,1,0:T(8,128)(2,1)}, u32[]{:S(2)}) copy-start(bf16[1,256,128]{2,1,0:T(8,128)(2,1)} %param.22) | copy-start | bytes 196612
  4.9 3.2 %copy-start.3 = (bf16[1,256,128]{2,1,0:T(8,128)(2,1)S(1)}, bf16[1,256,128]{2,1,0:T(8,128)(2,1)}, u32[]{:S(2)}) copy-start(bf16[1,256,128]{2,1,0:T(8,128)(2,1)} %param.23) | copy-start | bytes 196612
  4.9 3.2 %copy-start.4 = (f32[1,3072]{1,0:T(1,128)S(1)}, f32[1,3072]{1,0:T(1,128)}, u32[]{:S(2)}) copy-start(f32[1,3072]{1,0:T(1,128)} %shift_in.1) | copy-start | bytes 36868
  4.9 3.2 %copy-start.5 = (f32[1,3072]{1,0:T(1,128)S(1)}, f32[1,3072]{1,0:T(1,128)}, u32[]{:S(2)}) copy-start(f32[1,3072]{1,0:T(1,128)} %scale_in.1) | copy-start | bytes 36868
  4.9 3.2 %copy-start.6 = (f32[1,3072]{1,0:T(1,128)S(1)}, f32[1,3072]{1,0:T(1,128)}, u32[]{:S(2)}) copy-start(f32[1,3072]{1,0:T(1,128)} %gate_in.1) | copy-start | bytes 36868
  4.9 3.2 %copy-start.7 = (s32[256]{0:T(256)S(1)}, s32[256]{0:T(256)}, u32[]{:S(2)}) copy-start(s32[256]{0:T(256)} %param.13) | copy-start | bytes 3076
  4.9 3.2 %copy-start.8 = (s32[4]{0:T(128)S(1)}, s32[4]{0:T(128)}, u32[]{:S(2)}) copy-start(s32[4]{0:T(128)} %order.1) | copy-start | bytes 52
  5.0 3.2 %copy-start.9 = (f32[1,128]{1,0:T(1,128)S(1)}, f32[1,128]{1,0:T(1,128)}, u32[]{:S(2)}) copy-start(f32[1,128]{1,0:T(1,128)} %q_gain_in.1) | copy-start | bytes 1540
  5.0 3.2 %copy-start.10 = (f32[1,128]{1,0:T(1,128)S(1)}, f32[1,128]{1,0:T(1,128)}, u32[]{:S(2)}) copy-start(f32[1,128]{1,0:T(1,128)} %k_gain_in.1) | copy-start | bytes 1540
  8.2 1.4 %copy-start = (bf16[256,3072]{1,0:T(8,128)(2,1)S(1)}, bf16[256,3072]{1,0:T(8,128)(2,1)}, u32[]{:S(2)}) copy-start(bf16[256,3072]{1,0:T(8,128)(2,1)} %hidden.1) | copy-start | bytes 4718596

commit v4 on v3

--- a/solution.py
+++ b/solution.py
@@ -17,7 +17,7 @@
     members,
     patches,
     order,
-    weights,
+    weights_in,
     hidden,
     out_rows,
     shift_in,
@@ -31,6 +31,7 @@
     result,
     new_keys,
     new_values,
+    weights,
     raw,
     state,
     pick,
@@ -52,6 +53,7 @@
     updated,
     landed,
     load_sem,
+    wide_sem,
     raw_sem,
     w_send,
     w_recv,
@@ -124,6 +126,13 @@
         )
     ]
 
+    wide_loads = [
+        pltpu.make_async_copy(
+            weights_in.at[j], weights.at[:, pl.ds(j * head, head)], wide_sem.at[j]
+        )
+        for j in range(3)
+    ]
+
     def load_raw(k):
         return pltpu.make_async_copy(columns(hidden, k), raw.at[k], raw_sem.at[k])
 
@@ -134,6 +143,9 @@
     def _():
         for k in range(members):
             load_raw(k).start()
+
+    for copy in wide_loads:
+        copy.start()
 
     barrier = pltpu.get_barrier_semaphore()
 
@@ -244,6 +256,9 @@
     def _():
         for k in range(members):
             load_raw(k).wait()
+
+    for copy in wide_loads:
+        copy.wait()
 
     def gain(data, factor):
         square = jnp.mean(data * data, axis=-1, keepdims=True)
@@ -486,9 +501,10 @@
             jax.ShapeDtypeStruct((tokens, head), bf16),
             jax.ShapeDtypeStruct((tokens, head), bf16),
         ),
-        in_specs=[pl.BlockSpec(memory_space=pltpu.SMEM), inside] + [pl.BlockSpec(memory_space=pl.ANY)] * 10,
+        in_specs=[pl.BlockSpec(memory_space=pltpu.SMEM)] + [pl.BlockSpec(memory_space=pltpu.HBM)] * 11,
         out_specs=(inside, inside, inside),
         scratch_shapes=[
+            pltpu.VMEM((width, 3 * head), bf16),
             pltpu.VMEM((members, tokens, part), bf16),
             pltpu.VMEM((members, tokens, part), bf16),
             pltpu.VMEM((tokens, tokens), bf16),
@@ -503,6 +519,7 @@
             pltpu.VMEM((tokens, part), bf16),
             pltpu.VMEM((members, mine, part), bf16),
             dma((9,)),
+            dma((3,)),
             dma((members,)),
             dma((members,)),
             dma((members,)),
@@ -518,14 +535,14 @@
             dma((members,)),
         ],
         compiler_params=pltpu.CompilerParams(
-            collective_id=0, has_side_effects=True, vmem_limit_bytes=40 * 2**20
+            collective_id=0, has_side_effects=True, vmem_limit_bytes=60 * 2**20
         ),
         cost_estimate=pl.CostEstimate(
             flops=2 * tokens * width * 4 * head, bytes_accessed=10**7, transcendentals=tokens * tokens
         ),
     )(
         order,
-        w_qkv[0].reshape(width, 3 * head),
+        w_qkv[0].transpose(1, 0, 2),
         blocks(hidden_in),
         blocks(w_out[0]),
         blocks(mod_shift),

time: 96.6 us -> 86.3 us (0.89)
  local copies, waits for them, and re-layouts: 10.7 us -> 4.56 us
  Pallas kernels: 84.8 us -> 80.6 us
    pallas_call x1, Pallas kernels: 84.8 us -> 80.6 us  [per_device(): pl.pallas_call(functools.partial(kernel, segments, members, patches), out...]
    unnamed x26 -> x3, local copies, waits for them, and re-layouts: 7.65 us -> 4.56 us
    another operation x1 -> x0, local copies, waits for them, and re-layouts: 3.06 us -> none  [per_device(): w_qkv[0].reshape(width, 3 * head)]
where the time goes in v4:
time: 86.3 us; the launch traced here: 85.8 us
  Pallas kernels  80.6 us (93%)
  local copies, waits for them, and re-layouts  4.56 us (5%)
    pallas_call x1, Pallas kernels, per_device(): pl.pallas_call(functools.partial(kernel, segments, members, patches), out...  80.6 us
    unnamed x3, local copies, waits for them, and re-layouts  4.56 us

profile of v4, /device:TPU:4, one launch (start us, length us, event | category | flops | bytes accessed | tf_op | source)
XLA Modules:
  0.0 85.8 jit_solution(12322265951989565139)
XLA Ops:
  0.6 80.6 %shard_map.139 = (bf16[32,3072]{1,0:T(8,128)(2,1)}, bf16[256,128]{1,0:T(8,128)(2,1)}, bf16[256,128]{1,0:T(8,128)(2,1)}) custom-call(s32[4]{0:T(128)} %order.1, bf16[3,3072,128]{2,1,0:T(8,128)(2,1)} %bitcast.10, bf16[256,3072]{1,0:T(8,128)(2,1)} %hidden.1, bf16[128,3072]{1,0:T(8,128)(2,1)} %bitcast.11, f32[1,3072]{1,0:T(1,128)} %shift_in.1, ...), custom_call_target="tpu_custom_call" | custom-call | flops 805306368 | bytes 10000000 | tf_op jit(solution)/shard_map/pallas_call | solution.py:497
  81.2 1.6 %copy.18 = bf16[1,4,8,3072]{3,2,1,0:T(8,128)(2,1)} copy(bf16[1,4,8,3072]{3,2,1,0:T(8,128)(2,1)} %bitcast.12) | data formatting | bytes 393216
  82.9 1.5 %copy.19 = bf16[1,256,128]{2,1,0:T(8,128)(2,1)} copy(bf16[1,256,128]{2,1,0:T(8,128)(2,1)} %bitcast.16) | data formatting | bytes 131072
  84.3 1.5 %copy.20 = bf16[1,256,128]{2,1,0:T(8,128)(2,1)} copy(bf16[1,256,128]{2,1,0:T(8,128)(2,1)} %bitcast.15) | data formatting | bytes 131072

commit v5 on v4

--- a/solution.py
+++ b/solution.py
@@ -309,6 +309,27 @@
 
     lax.fori_loop(0, CHUNKS, project, 0)
 
+    def heads(origin, r):
+        return attended.at[
+            pl.ds(pl.multiple_of(r * chunk, chunk), chunk),
+            pl.ds(pl.multiple_of(origin * head, head), head),
+        ]
+
+    def a_copy(step, r):
+        place = heads(me, r)
+        return remote(place, place, a_send.at[step, r], a_recv.at[me, r], slow_peer(step) * fast + b)
+
+    def a_forward(origin_slow, step, r):
+        origin = origin_slow * fast + b
+        place = heads(origin, r)
+        return remote(
+            place, place, a_pass.at[origin_slow, step, r], a_recv.at[origin, r], a * fast + fast_peer(step)
+        )
+
+    def a_arrival(origin, r):
+        place = heads(origin, r)
+        return remote(place, place, a_send.at[0, r], a_recv.at[origin, r], other(1))
+
     def attend(r, carry):
         rows = pl.ds(pl.multiple_of(r * chunk, chunk), chunk)
         asking = lax.broadcasted_iota(jnp.int32, (chunk, tokens), 0) + r * chunk
@@ -329,32 +350,13 @@
             jnp.dot(fresh, values[...], preferred_element_type=jnp.float32)
             + jnp.dot(stale, old_values[...], preferred_element_type=jnp.float32)
         ).astype(jnp.bfloat16)
+        for step in range(1, slow):
+            a_copy(step, r).start()
+        for hop in range(1, fast):
+            a_forward(a, hop, r).start()
         return carry
 
     lax.fori_loop(0, CHUNKS, attend, 0)
-
-    def heads(origin):
-        return attended.at[:, pl.ds(pl.multiple_of(origin * head, head), head)]
-
-    def a_copy(step):
-        place = heads(me)
-        return remote(place, place, a_send.at[step], a_recv.at[me], slow_peer(step) * fast + b)
-
-    def a_forward(origin_slow, step):
-        origin = origin_slow * fast + b
-        place = heads(origin)
-        return remote(
-            place, place, a_pass.at[origin_slow, step], a_recv.at[origin], a * fast + fast_peer(step)
-        )
-
-    def a_arrival(origin):
-        place = heads(origin)
-        return remote(place, place, a_send.at[0], a_recv.at[origin], other(1))
-
-    for step in range(1, slow):
-        a_copy(step).start()
-    for hop in range(1, fast):
-        a_forward(a, hop).start()
 
     back = (((0,), (0,)), ((), ()))
     new_keys[...] = lax.dot_general(
@@ -364,17 +366,17 @@
         pick[...], values[...], back, preferred_element_type=jnp.float32
     ).astype(jnp.bfloat16)
 
-    for step in range(1, slow):
-        origin_slow = slow_peer(step)
-        a_arrival(origin_slow * fast + b).wait_recv()
-        for hop in range(1, fast):
-            a_forward(origin_slow, hop).start()
+    def pass_on(r):
+        for step in range(1, slow):
+            origin_slow = slow_peer(step)
+            a_arrival(origin_slow * fast + b, r).wait_recv()
+            for hop in range(1, fast):
+                a_forward(origin_slow, hop, r).start()
+
     for step in range(1, members):
         w_arrival(step).wait_recv()
         twin_copy(step, core).start()
-    for hop in range(1, fast):
-        for step in range(slow):
-            a_arrival(slow_peer(step) * fast + fast_peer(hop)).wait_recv()
+    pass_on(0)
     for step in range(1, members):
         twin_copy(step, 1 - core).wait_recv()
     my_gate = gate[:, pl.ds(pl.multiple_of(me * part, 128), part)] if aligned else gate[me]
@@ -390,7 +392,35 @@
             section + 1,
         )
 
+    def o_copy(target):
+        return remote(
+            updated.at[pl.ds(pl.multiple_of(target * mine, mine), mine)],
+            landed.at[me],
+            o_send.at[target],
+            o_recv.at[me],
+            target,
+        )
+
+    def o_arrival(step):
+        origin = other(step)
+        return remote(landed.at[origin], landed.at[origin], o_send.at[origin], o_recv.at[origin], origin)
+
+    def o_start(r):
+        for i in range(members // CHUNKS):
+            target = r * (members // CHUNKS) + i
+
+            @pl.when(target != me)
+            def _():
+                o_copy(target).start()
+
     def finish(r, carry):
+        @pl.when(r + 1 < CHUNKS)
+        def _():
+            pass_on(r + 1)
+
+        for hop in range(1, fast):
+            for step in range(slow):
+                a_arrival(slow_peer(step) * fast + fast_peer(hop), r).wait_recv()
         rows = pl.ds(pl.multiple_of(r * chunk, chunk), chunk)
         branch = jnp.dot(attended[rows, :], out_cols[...], preferred_element_type=jnp.float32)
         updated[rows, :] = (state[me, rows].astype(jnp.float32) + my_gate * branch).astype(jnp.bfloat16)
@@ -400,38 +430,31 @@
             for step in range(slow):
                 s_copy(step, r).start()
 
+        @pl.when(last)
+        def _():
+            o_start(r)
+
         return carry
 
     lax.fori_loop(0, CHUNKS, finish, 0)
 
-    def o_copy(step):
-        target = other(step)
-        return remote(
-            updated.at[pl.ds(pl.multiple_of(target * mine, mine), mine)],
-            landed.at[me],
-            o_send.at[step],
-            o_recv.at[me],
-            target,
-        )
-
-    def o_arrival(step):
-        origin = other(step)
-        return remote(landed.at[origin], landed.at[origin], o_send.at[step], o_recv.at[origin], origin)
-
-    for step in range(1, members):
-        o_copy(step).start()
+    @pl.when(jnp.logical_not(last))
+    def _():
+        for r in range(CHUNKS):
+            o_start(r)
+
     landed[me] = updated[pl.ds(pl.multiple_of(me * mine, mine), mine), :]
 
     for step in range(1, members):
         w_copy(step).wait_send()
         twin_copy(step, core).wait_send()
-    for step in range(1, slow):
-        a_copy(step).wait_send()
-    for hop in range(1, fast):
-        for step in range(slow):
-            a_forward(slow_peer(step), hop).wait_send()
-
     def drain(r, carry):
+        for step in range(1, slow):
+            a_copy(step, r).wait_send()
+        for hop in range(1, fast):
+            for step in range(slow):
+                a_forward(slow_peer(step), hop, r).wait_send()
+
         @pl.when(jnp.logical_not(last))
         def _():
             for step in range(slow):
@@ -449,7 +472,7 @@
     for step in range(1, members):
         o_arrival(step).wait_recv()
     for step in range(1, members):
-        o_copy(step).wait_send()
+        o_copy(other(step)).wait_send()
     if aligned:
         for k in range(members):
             result[:, k * part : (k + 1) * part] = landed[k]
@@ -525,9 +548,9 @@
             dma((members,)),
             dma((members,)),
             dma((members,)),
-            dma((slow,)),
-            dma((slow, fast)),
-            dma((members,)),
+            dma((slow, CHUNKS)),
+            dma((slow, fast, CHUNKS)),
+            dma((members, CHUNKS)),
             dma((slow, CHUNKS)),
             dma((slow, fast, CHUNKS)),
             dma((members, CHUNKS)),

time: 86.3 us -> 81.1 us (0.940); the launches traced: 85.8 us -> 79.7 us
  Pallas kernels: 80.6 us -> 74.5 us
    pallas_call x1, Pallas kernels: 80.6 us -> 74.5 us  [per_device(): pl.pallas_call(functools.partial(kernel, segments, members, patches), out...]
where the time goes in v5:
time: 81.1 us; the launch traced here: 79.7 us
  Pallas kernels  74.5 us (92%)
  local copies, waits for them, and re-layouts  4.56 us (6%)
    pallas_call x1, Pallas kernels, per_device(): pl.pallas_call(functools.partial(kernel, segments, members, patches), out...  74.5 us
    unnamed x3, local copies, waits for them, and re-layouts  4.56 us

profile of v5, /device:TPU:4, one launch (start us, length us, event | category | flops | bytes accessed | tf_op | source)
XLA Modules:
  0.0 79.7 jit_solution(7646258843384349019)
XLA Ops:
  0.6 74.5 %shard_map.139 = (bf16[32,3072]{1,0:T(8,128)(2,1)}, bf16[256,128]{1,0:T(8,128)(2,1)}, bf16[256,128]{1,0:T(8,128)(2,1)}) custom-call(s32[4]{0:T(128)} %order.1, bf16[3,3072,128]{2,1,0:T(8,128)(2,1)} %bitcast.10, bf16[256,3072]{1,0:T(8,128)(2,1)} %hidden.1, bf16[128,3072]{1,0:T(8,128)(2,1)} %bitcast.11, f32[1,3072]{1,0:T(1,128)} %shift_in.1, ...), custom_call_target="tpu_custom_call" | custom-call | flops 805306368 | bytes 10000000 | tf_op jit(solution)/shard_map/pallas_call | solution.py:520
  75.1 1.6 %copy.18 = bf16[1,4,8,3072]{3,2,1,0:T(8,128)(2,1)} copy(bf16[1,4,8,3072]{3,2,1,0:T(8,128)(2,1)} %bitcast.12) | data formatting | bytes 393216
  76.7 1.5 %copy.19 = bf16[1,256,128]{2,1,0:T(8,128)(2,1)} copy(bf16[1,256,128]{2,1,0:T(8,128)(2,1)} %bitcast.16) | data formatting | bytes 131072
  78.2 1.5 %copy.20 = bf16[1,256,128]{2,1,0:T(8,128)(2,1)} copy(bf16[1,256,128]{2,1,0:T(8,128)(2,1)} %bitcast.15) | data formatting | bytes 131072

commit v6 on v5

--- a/solution.py
+++ b/solution.py
@@ -267,14 +267,24 @@
     def vector(ref, k):
         return ref[:, k * part : (k + 1) * part] if aligned else ref[k]
 
+    def pass_state(r):
+        for step in range(slow):
+            origin_slow = slow_peer(step)
+            s_arrival(origin_slow * fast + b, r).wait_recv()
+            for hop in range(1, fast):
+                s_forward(origin_slow, hop, r).start()
+
+    @pl.when(jnp.logical_not(first))
+    def _():
+        pass_state(0)
+
     def project(r, carry):
+        @pl.when(jnp.logical_and(jnp.logical_not(first), r + 1 < CHUNKS))
+        def _():
+            pass_state(r + 1)
+
         @pl.when(jnp.logical_not(first))
         def _():
-            for step in range(slow):
-                origin_slow = slow_peer(step)
-                s_arrival(origin_slow * fast + b, r).wait_recv()
-                for hop in range(1, fast):
-                    s_forward(origin_slow, hop, r).start()
             for hop in range(1, fast):
                 for step in range(slow):
                     s_arrival(slow_peer(step) * fast + fast_peer(hop), r).wait_recv()

time: 81.1 us -> 75.1 us (0.926)
  Pallas kernels: 74.5 us -> 68.6 us
    pallas_call x1, Pallas kernels: 74.5 us -> 68.6 us  [per_device(): pl.pallas_call(functools.partial(kernel, segments, members, patches), out...]
where the time goes in v6:
time: 75.1 us; the launch traced here: 73.8 us
  Pallas kernels  68.6 us (91%)
  local copies, waits for them, and re-layouts  4.56 us (6%)
    pallas_call x1, Pallas kernels, per_device(): pl.pallas_call(functools.partial(kernel, segments, members, patches), out...  68.6 us
    unnamed x3, local copies, waits for them, and re-layouts  4.56 us

profile of v6, /device:TPU:4, one launch (start us, length us, event | category | flops | bytes accessed | tf_op | source)
XLA Modules:
  0.0 73.8 jit_solution(7825559660297246456)
XLA Ops:
  0.6 68.6 %shard_map.139 = (bf16[32,3072]{1,0:T(8,128)(2,1)}, bf16[256,128]{1,0:T(8,128)(2,1)}, bf16[256,128]{1,0:T(8,128)(2,1)}) custom-call(s32[4]{0:T(128)} %order.1, bf16[3,3072,128]{2,1,0:T(8,128)(2,1)} %bitcast.10, bf16[256,3072]{1,0:T(8,128)(2,1)} %hidden.1, bf16[128,3072]{1,0:T(8,128)(2,1)} %bitcast.11, f32[1,3072]{1,0:T(1,128)} %shift_in.1, ...), custom_call_target="tpu_custom_call" | custom-call | flops 805306368 | bytes 10000000 | tf_op jit(solution)/shard_map/pallas_call | solution.py:530
  69.3 1.6 %copy.18 = bf16[1,4,8,3072]{3,2,1,0:T(8,128)(2,1)} copy(bf16[1,4,8,3072]{3,2,1,0:T(8,128)(2,1)} %bitcast.12) | data formatting | bytes 393216
  70.9 1.5 %copy.19 = bf16[1,256,128]{2,1,0:T(8,128)(2,1)} copy(bf16[1,256,128]{2,1,0:T(8,128)(2,1)} %bitcast.16) | data formatting | bytes 131072
  72.4 1.5 %copy.20 = bf16[1,256,128]{2,1,0:T(8,128)(2,1)} copy(bf16[1,256,128]{2,1,0:T(8,128)(2,1)} %bitcast.15) | data formatting | bytes 131072
